TPU v7x, 512 devices: a whole 4x4x16 slice. The times are simulated.
512 devices in a mesh: space: 64 (over x, z), member: 8 (over y, core).
Axes of the slice: x: 4, y: 4, z: 16, core: 2. Of those that a mesh axis runs over, the one named last changes fastest.
Arguments:
- prior_ensemble: bfloat16 [256, 1024, 1024], P('member', 'space'), may hold values from -6 to 6
- measured_location: int32 [8, 128, 128], P('member', 'space'), may hold values from 0 to 2047
- measurements_per_tile: int32 [8, 128], P('member', 'space'), may hold values from 32 to 128
- measured_datum: float32 [8, 128, 128], P('member', 'space'), may hold values from -6 to 6
- measurement_perturb_draws: bfloat16 [8, 256, 128, 128], P('member', None, 'space'), may hold values from -5 to 5
- measurement_error_spread: float32 [8, 128, 128], P('member', 'space'), may hold values from 0.5 to 2
Outputs:
- increment: bfloat16 [256, 1024, 1024], P('member', 'space')
Inputs may be any that keep to these rules, and one draw needn't show every extreme that they name: measured_location numbers a cell of its region row by row: 128 cells a row, 16 rows.
All inputs are finite; a program needn't handle non-finite values.
Results may differ from a plain program's by a relative error of at most 0.006.
Values may be sent and summed in bfloat16 or wider, within the bound.
A program may use at most 64 MiB of HBM per device.

v0:
```python
import math

import jax
import jax.numpy as jnp
from jax import lax
from jax.sharding import PartitionSpec as P

LOC = 4
ITERS = 3


def extended(block, sides, width):
    for axis, dim in sides:
        count = lax.axis_size(axis)
        forward = [(i, i + 1) for i in range(count - 1)]
        backward = [(target, source) for source, target in forward]
        low = lax.ppermute(
            lax.slice_in_dim(block, block.shape[dim] - width, None, axis=dim), axis, forward
        )
        high = lax.ppermute(lax.slice_in_dim(block, 0, width, axis=dim), axis, backward)
        block = jnp.concatenate([low, block, high], axis=dim)
    return block


def taper_weight(rows_left, cols_left, rows_right, cols_right):
    row_gap = rows_left[:, None] - rows_right[None, :]
    col_gap = cols_left[:, None] - cols_right[None, :]
    distance = row_gap * row_gap + col_gap * col_gap
    return jnp.where(
        distance < 9.0 * LOC * LOC,
        jnp.exp(-0.5 * distance / (LOC * LOC)),
        jnp.zeros((), distance.dtype),
    )


def reduce_dots(columns):
    return lax.psum(columns, ("space", "member"))


def covariance_apply(vector, variance, kernel, obs_dev):
    members = vector.shape[0]
    vector_near = extended(
        vector.reshape(members, 1, 1, obs_dev), (("space", 1), ("member", 2)), 1
    ).reshape(members, 9 * obs_dev)
    product = lax.dot_general(
        vector_near,
        kernel,
        (((1,), (1,)), ((), ())),
        precision=lax.Precision.HIGHEST,
        preferred_element_type=jnp.float32,
    )
    return (variance[None, :] * vector + product, vector_near)


def shards(
    prior_ensemble,
    measured_location,
    measurements_per_tile,
    measured_datum,
    measurement_perturb_draws,
    measurement_error_spread,
):
    strip_estimate = lax.all_to_all(
        prior_ensemble, "member", split_axis=2, concat_axis=0, tiled=True
    )
    member_mean = jnp.mean(strip_estimate, axis=0, dtype=jnp.float32)
    xprime = (strip_estimate.astype(jnp.float32) - member_mean).astype(jnp.bfloat16)
    members, row_dev, col_sub = strip_estimate.shape
    cell_count = row_dev * col_sub
    block_size = measured_location.shape[2]
    obs_dev = measured_location.shape[1] * block_size
    slab_flat = strip_estimate.reshape(members, cell_count)
    xp_flat = xprime.reshape(members, cell_count)
    obs_cells = measured_location.reshape(obs_dev)
    slot_index = jnp.arange(obs_dev, dtype=jnp.int32) % block_size
    slot_counts = jnp.repeat(measurements_per_tile.reshape(-1), block_size)
    active = slot_index < slot_counts
    x_obs = jnp.take(slab_flat, obs_cells, axis=1).astype(jnp.float32)
    y_pert = jnp.where(
        active[None, :], jnp.take(xp_flat, obs_cells, axis=1), jnp.zeros((), jnp.bfloat16)
    )
    variance = measurement_error_spread.reshape(obs_dev)
    noise_obs = measurement_perturb_draws.reshape(members, obs_dev).astype(jnp.float32)
    values_obs = measured_datum.reshape(obs_dev)
    innovation = jnp.where(
        active[None, :],
        values_obs[None, :] + jnp.sqrt(variance)[None, :] * noise_obs - x_obs,
        jnp.zeros((), jnp.float32),
    )
    obs_rows = (obs_cells // col_sub).astype(jnp.float32)
    obs_cols = (obs_cells % col_sub).astype(jnp.float32)
    positions = jnp.stack([obs_rows, obs_cols]).astype(jnp.bfloat16)
    y_near, pos_near = (
        extended(y_pert.reshape(members, 1, 1, obs_dev), (("space", 1), ("member", 2)), 1),
        extended(positions.reshape(2, 1, 1, obs_dev), (("space", 1), ("member", 2)), 1),
    )
    y_near = y_near.reshape(members, 9 * obs_dev)
    pos_near = pos_near.reshape(2, 9 * obs_dev)
    piece_index = jnp.arange(9 * obs_dev, dtype=jnp.int32) // obs_dev
    shift_rows = (piece_index // 3 - 1).astype(jnp.float32) * row_dev
    shift_cols = (piece_index % 3 - 1).astype(jnp.float32) * col_sub
    near_rows = pos_near[0].astype(jnp.float32) + shift_rows
    near_cols = pos_near[1].astype(jnp.float32) + shift_cols
    cross_sum = lax.dot_general(
        y_pert, y_near, (((0,), (0,)), ((), ())), preferred_element_type=jnp.float32
    )
    kernel = cross_sum * taper_weight(obs_rows, obs_cols, near_rows, near_cols) / (members - 1)
    z_near = jnp.zeros((members, 9 * obs_dev), jnp.float32)
    residual = innovation
    direction = innovation
    norm_now = reduce_dots(jnp.sum(residual * residual, axis=1)[None, :])[0]
    for sweep_index in range(ITERS):
        applied, direction_near = covariance_apply(direction, variance, kernel, obs_dev)
        curvature = reduce_dots(jnp.sum(direction * applied, axis=1)[None, :])[0]
        step_size = norm_now / curvature
        z_near = z_near + step_size[:, None] * direction_near
        if sweep_index + 1 < ITERS:
            residual = residual - step_size[:, None] * applied
            norm_next = reduce_dots(jnp.sum(residual * residual, axis=1)[None, :])[0]
            direction = residual + (norm_next / norm_now)[:, None] * direction
            norm_now = norm_next
    weights_z = z_near.astype(jnp.bfloat16)
    block_cells = math.gcd(cell_count, 512)

    def add_block(block_index, buffer):
        offset = block_index * block_cells
        xp_block = lax.dynamic_slice_in_dim(xp_flat, offset, block_cells, 1)
        covariance = lax.dot_general(
            xp_block, y_near, (((0,), (0,)), ((), ())), preferred_element_type=jnp.float32
        )
        cell_index = offset + jnp.arange(block_cells, dtype=jnp.int32)
        rows_block = (cell_index // col_sub).astype(jnp.float32)
        cols_block = (cell_index % col_sub).astype(jnp.float32)
        weight_tile = (
            covariance * taper_weight(rows_block, cols_block, near_rows, near_cols) / (members - 1)
        ).astype(jnp.bfloat16)
        update = lax.dot_general(
            weights_z, weight_tile, (((1,), (1,)), ((), ())), preferred_element_type=jnp.float32
        ).astype(jnp.bfloat16)
        return lax.dynamic_update_slice_in_dim(buffer, update, offset, 1)

    increment = lax.fori_loop(
        0, cell_count // block_cells, add_block, jnp.zeros((members, cell_count), jnp.bfloat16)
    )
    increment = increment.reshape(members, row_dev, col_sub)
    return lax.all_to_all(increment, "member", split_axis=0, concat_axis=2, tiled=True)


def solution(mesh):
    in_specs = (
        P("member", "space", None),
        P("member", "space", None),
        P("member", "space"),
        P("member", "space", None),
        P("member", None, "space", None),
        P("member", "space", None),
    )
    out_specs = P("member", "space", None)
    return jax.shard_map(shards, mesh=mesh, in_specs=in_specs, out_specs=out_specs, check_vma=False)
```

profile of v0, /device:TPU:1, one launch (start us, length us, event | category | flops | bytes accessed | tf_op | source)
XLA Modules:
  0.0 720.1 jit_solution(1101632747385398282)
XLA Ops:
  0.0 7.4 %copy.47 = bf16[32,16,1024]{0,1,2:T(8,128)(2,1)} copy(bf16[32,16,1024]{2,1,0:T(8,128)(2,1)} %param.10) | data formatting | bytes 2097152 | tf_op args[0]
  7.4 7.9 %reshape.477 = bf16[8,2,32768]{2,1,0:T(2,128)(2,1)} reshape(bf16[1024,16,32]{2,1,0:T(8,128)(2,1)} %bitcast.119) | data formatting | bytes 2097152
  15.3 10.5 %all-to-all-start = ((bf16[8,2,32768]{2,1,0:T(2,128)(2,1)}), bf16[8,2,32768]{2,1,0:T(2,128)(2,1)S(1)}, u32[]{:S(2)}, u32[]{:S(2)}) async-start(bf16[8,2,32768]{2,1,0:T(2,128)(2,1)} %reshape.477), calls=%async_computation | async-start | bytes 2097152 | tf_op jit(solution)/shard_map/all_to_all | solution.py:63
  25.8 1.3 collective-permute-start.4
  27.1 1.3 collective-permute-start.5
  28.7 12.2 %all-to-all-done = bf16[8,2,32768]{2,1,0:T(2,128)(2,1)S(1)} async-done(((bf16[8,2,32768]{2,1,0:T(2,128)(2,1)}), bf16[8,2,32768]{2,1,0:T(2,128)(2,1)S(1)}, u32[]{:S(2)}, u32[]{:S(2)}) %all-to-all-start) | async-done | bytes 1048608 | tf_op jit(solution)/shard_map/all_to_all | solution.py:63
  40.9 4.5 reshape.478
  45.4 5.4 copy.48
  52.2 1.2 gather_fusion
  53.5 1.3 collective-permute-start
  54.8 1.3 collective-permute-start.1
  56.1 1.2 gather_fusion.1
  57.5 4.0 collective-permute-start.8
  61.5 1.3 collective-permute-start.9
  62.8 3.5 collective-permute-start.6
  67.1 1.9 collective-permute-start.7
  69.0 3.6 collective-permute-done.7
  73.5 1.9 collective-permute-start.2
  75.4 2.4 collective-permute-start.3
  78.8 3.2 collective-permute-start.10
  81.9 2.0 collective-permute-start.11
  84.9 1.1 fusion.20
  86.0 5.1 collective-permute-done.10
  91.2 4.4 collective-permute-done.11
  95.6 1.6 pad_maximum_fusion
  97.2 2.2 multiply_reduce_fusion.3
  99.4 108.2 %all-reduce = (f32[1,256]{1,0:T(1,128)S(1)}, f32[1,256]{1,0:T(1,128)S(1)}) all-reduce(f32[1,256]{1,0:T(1,128)S(1)} %bitcast.155, f32[1,256]{1,0:T(1,128)S(1)} %bitcast.154), channel_id=1, replica_groups=mesh['space'=64,'member'=8] {'space','member'}, use_global_device_ids=true, to_apply=%region_2.4 | all-reduce | flops 512 | bytes 4096 | tf_op jit(solution)/shard_map/psum | solution.py:37
  208.1 100.5 %psum.44 = f32[1,256]{1,0:T(1,128)S(1)} all-reduce(f32[1,256]{1,0:T(1,128)S(1)} %bitcast.150), channel_id=1, replica_groups=mesh['space'=64,'member'=8] {'space','member'}, use_global_device_ids=true, to_apply=%region_6.8 | all-reduce | flops 256 | bytes 2048 | tf_op jit(solution)/shard_map/psum | solution.py:37
  308.7 2.9 collective-permute-start.12
  311.6 1.3 collective-permute-start.13
  312.9 3.6 collective-permute-done.12
  316.5 3.8 collective-permute-done.13
  320.4 4.6 collective-permute-start.14
  325.0 1.9 collective-permute-start.15
  326.9 7.0 collective-permute-done.14
  333.9 4.4 collective-permute-done.15
  338.5 2.2 multiply_reduce_fusion.1
  340.7 101.4 %psum.45 = f32[1,256]{1,0:T(1,128)S(1)} all-reduce(f32[1,256]{1,0:T(1,128)S(1)} %bitcast.151), channel_id=1, replica_groups=mesh['space'=64,'member'=8] {'space','member'}, use_global_device_ids=true, to_apply=%region_8.10 | all-reduce | flops 256 | bytes 2048 | tf_op jit(solution)/shard_map/psum | solution.py:37
  442.2 98.7 %psum.46 = f32[1,256]{1,0:T(1,128)S(1)} all-reduce(f32[1,256]{1,0:T(1,128)S(1)} %bitcast.152), channel_id=1, replica_groups=mesh['space'=64,'member'=8] {'space','member'}, use_global_device_ids=true, to_apply=%region_10.12 | all-reduce | flops 256 | bytes 2048 | tf_op jit(solution)/shard_map/psum | solution.py:37
  540.9 3.8 collective-permute-start.16
  544.8 1.3 collective-permute-start.17
  546.1 3.6 collective-permute-done.16
  549.7 3.8 collective-permute-done.17
  553.5 1.1 pad_maximum_fusion.6
  554.6 4.4 collective-permute-start.18
  559.0 1.9 collective-permute-start.19
  561.0 1.6 copy.56
  562.5 3.1 copy.52
  565.6 3.1 copy.53
  568.8 3.9 collective-permute-done.19
  572.7 1.6 pad_maximum_fusion.2
  574.3 1.5 copy-done.2
  575.7 2.3 fusion.23
  578.0 3.2 copy.54
  581.2 100.9 %psum.47 = f32[1,256]{1,0:T(1,128)S(1)} all-reduce(f32[1,256]{1,0:T(1,128)S(1)} %bitcast.149), channel_id=1, replica_groups=mesh['space'=64,'member'=8] {'space','member'}, use_global_device_ids=true, to_apply=%region_12.14 | all-reduce | flops 256 | bytes 2048 | tf_op jit(solution)/shard_map/psum | solution.py:37
  682.1 2.9 add_convert_fusion
  685.1 14.4 %while.15 = (s32[]{:T(128)}, bf16[256,2048]{0,1:T(8,128)(2,1)S(1)}, bf16[256,2048]{0,1:T(8,128)(2,1)}, bf16[256,2304]{1,0:T(8,128)(2,1)}, f32[2304]{0:T(1024)S(1...) while((s32[]{:T(128)}, bf16[256,2048]{0,1:T(8,128)(2,1)S(1)}, ...), condition=%wide.region_14.16_spmd, body=%wide.region_13.15_spmd.sunk | while | flops 1221078016 | bytes 2917535 | solution.py:142
  685.2 3.6 fusion.71
  688.8 3.6 fusion.71
  692.4 3.6 fusion.71
  696.0 3.6 fusion.71
  699.6 1.1 copy.59
  700.7 18.2 %all_to_all.36 = bf16[256,16,128]{2,1,0:T(8,128)(2,1)S(1)} all-to-all(bf16[256,16,128]{2,1,0:T(8,128)(2,1)S(1)} %copy.59), channel_id=1, replica_groups=mesh['space'=64,'member'=8] {'member'}, dimensions={0} | all-to-all | bytes 2097152 | tf_op jit(solution)/shard_map/all_to_all | solution.py:146
  718.9 1.3 copy.66
  (93 shorter events, 6.5 us)
Async XLA Ops:
  7.4 18.4 %copy-start.19 = (s32[1,2,128]{2,1,0:T(2,128)S(1)}, s32[1,2,128]{2,1,0:T(2,128)}, u32[]{:S(2)}) copy-start(s32[1,2,128]{2,1,0:T(2,128)} %param.11) | copy-start | bytes 3076
  7.4 21.0 %copy-start.13 = (bf16[1,256,2,128]{3,2,1,0:T(2,128)(2,1)S(1)}, bf16[1,256,2,128]{3,2,1,0:T(2,128)(2,1)}, u32[]{:S(2)}) copy-start(bf16[1,256,2,128]{3,2,1,0:T(2,128)(2,1)} %param.14) | copy-start | bytes 393220
  15.3 13.3 %copy-start.14 = (f32[1,2,128]{2,1,0:T(2,128)S(1)}, f32[1,2,128]{2,1,0:T(2,128)}, u32[]{:S(2)}) copy-start(f32[1,2,128]{2,1,0:T(2,128)} %param.15) | copy-start | bytes 3076
  15.3 13.3 %copy-start.21 = (s32[1,2]{1,0:T(1,128)S(1)}, s32[1,2]{1,0:T(1,128)}, u32[]{:S(2)}) copy-start(s32[1,2]{1,0:T(1,128)} %param.12) | copy-start | bytes 28
  15.3 25.6 %all-to-all-start = ((bf16[8,2,32768]{2,1,0:T(2,128)(2,1)}), bf16[8,2,32768]{2,1,0:T(2,128)(2,1)S(1)}, u32[]{:S(2)}, u32[]{:S(2)}) async-start(bf16[8,2,32768]{2,1,0:T(2,128)(2,1)} %reshape.477), calls=%async_computation | async-start | bytes 2097152 | tf_op jit(solution)/shard_map/all_to_all | solution.py:63
  25.8 35.7 %collective-permute-start.4 = (bf16[2,1,1,256]{3,2,1,0:T(2,128)(2,1)S(1)}, bf16[2,1,1,256]{3,2,1,0:T(2,128)(2,1)S(1)}, u32[]{:S(2)}, u32[]{:S(2)}) collective-permute-start(bf16[2,1,1,256]{3,2,1,0:T(2,128)(2,1)S(1)} %pad_maximum_fusion.10), channel_id=1, source_target_pairs={{0,8},{8,16},{16,24},{24,32},{32,40},{40,48},{48,56},{56,64},{64,7... | collective-permute-start | bytes 3080 | tf_op jit(solution)/shard_map/ppermute | solution.py:17
  27.1 35.7 %collective-permute-start.5 = (bf16[2,1,1,256]{3,2,1,0:T(2,128)(2,1)S(1)}, bf16[2,1,1,256]{3,2,1,0:T(2,128)(2,1)S(1)}, u32[]{:S(2)}, u32[]{:S(2)}) collective-permute-start(bf16[2,1,1,256]{3,2,1,0:T(2,128)(2,1)S(1)} %pad_maximum_fusion.10), channel_id=1, source_target_pairs={{8,0},{16,8},{24,16},{32,24},{40,32},{48,40},{56,48},{64,56},{72,6... | collective-permute-start | bytes 3080 | tf_op jit(solution)/shard_map/ppermute | solution.py:20
  51.8 5.4 copy-start.20
  52.2 26.6 %copy-start.6 = (bf16[256,2048]{0,1:T(8,128)(2,1)}, bf16[256,2048]{0,1:T(8,128)(2,1)S(1)}, u32[]{:S(2)}) copy-start(bf16[256,2048]{0,1:T(8,128)(2,1)S(1)} %subtract_convert_fusion) | copy-start | bytes 3145732
  53.5 19.1 %collective-permute-start = (bf16[256,1,1,256]{0,3,2,1:T(8,128)(2,1)S(1)}, bf16[256,1,1,256]{0,3,2,1:T(8,128)(2,1)S(1)}, u32[]{:S(2)}, u32[]{:S(2)}) collective-permute-start(bf16[256,1,1,256]{0,3,2,1:T(8,128)(2,1)S(1)} %fusion.52), channel_id=1, source_target_pairs={{0,8},{8,16},{16,24},{24,32},{32,40},{40,48},{48,56},{56,64},{64,7... | collective-permute-start | bytes 393224 | tf_op jit(solution)/shard_map/ppermute | solution.py:17
  54.8 17.8 %collective-permute-start.1 = (bf16[256,1,1,256]{0,3,2,1:T(8,128)(2,1)S(1)}, bf16[256,1,1,256]{0,3,2,1:T(8,128)(2,1)S(1)}, u32[]{:S(2)}, u32[]{:S(2)}) collective-permute-start(bf16[256,1,1,256]{0,3,2,1:T(8,128)(2,1)S(1)} %fusion.52), channel_id=1, source_target_pairs={{8,0},{16,8},{24,16},{32,24},{40,32},{48,40},{56,48},{64,56},{72,6... | collective-permute-start | bytes 393224 | tf_op jit(solution)/shard_map/ppermute | solution.py:20
  57.5 20.3 %collective-permute-start.8 = (f32[256,1,1,256]{0,3,2,1:T(8,128)S(1)}, f32[256,1,1,256]{0,3,2,1:T(8,128)S(1)}, u32[]{:S(2)}, u32[]{:S(2)}) collective-permute-start(f32[256,1,1,256]{0,3,2,1:T(8,128)S(1)} %bitcast.121), channel_id=1, source_target_pairs={{0,8},{8,16},{16,24},{24,32},{32,40},{40,48},{48,56},{56,64},{64,7... | collective-permute-start | bytes 786440 | tf_op jit(solution)/shard_map/ppermute | solution.py:17
  61.5 16.3 %collective-permute-start.9 = (f32[256,1,1,256]{0,3,2,1:T(8,128)S(1)}, f32[256,1,1,256]{0,3,2,1:T(8,128)S(1)}, u32[]{:S(2)}, u32[]{:S(2)}) collective-permute-start(f32[256,1,1,256]{0,3,2,1:T(8,128)S(1)} %bitcast.122), channel_id=1, source_target_pairs={{8,0},{16,8},{24,16},{32,24},{40,32},{48,40},{56,48},{64,56},{72,6... | collective-permute-start | bytes 786440 | tf_op jit(solution)/shard_map/ppermute | solution.py:20
  62.8 4.3 collective-permute-start.6
  67.1 5.5 collective-permute-start.7
  73.5 10.6 %collective-permute-start.2 = (bf16[256,3,1,256]{0,3,2,1:T(8,128)(2,1)}, bf16[256,3,1,256]{0,3,2,1:T(8,128)(2,1)S(1)}, u32[]{:S(2)}, u32[]{:S(2)}) collective-permute-start(bf16[256,3,1,256]{0,3,2,1:T(8,128)(2,1)} %pad_maximum_fusion.7), channel_id=1, source_target_pairs={{0,1},{1,2},{2,3},{3,4},{4,5},{5,6},{6,7},{8,9},{9,10},{10,11},{11... | collective-permute-start | bytes 1179656 | tf_op jit(solution)/shard_map/ppermute | solution.py:17
  75.4 9.3 %collective-permute-start.3 = (bf16[256,3,1,256]{0,3,2,1:T(8,128)(2,1)}, bf16[256,3,1,256]{0,3,2,1:T(8,128)(2,1)S(1)}, u32[]{:S(2)}, u32[]{:S(2)}) collective-permute-start(bf16[256,3,1,256]{0,3,2,1:T(8,128)(2,1)} %pad_maximum_fusion.7), channel_id=1, source_target_pairs={{1,0},{2,1},{3,2},{4,3},{5,4},{6,5},{7,6},{9,8},{10,9},{11,10},{12... | collective-permute-start | bytes 1179656 | tf_op jit(solution)/shard_map/ppermute | solution.py:20
  78.8 12.4 %collective-permute-start.10 = (f32[256,3,1,256]{0,3,2,1:T(8,128)}, f32[256,3,1,256]{0,3,2,1:T(8,128)}, u32[]{:S(2)}, u32[]{:S(2)}) collective-permute-start(f32[256,3,1,256]{0,3,2,1:T(8,128)} %pad_maximum_fusion.4), channel_id=1, source_target_pairs={{0,1},{1,2},{2,3},{3,4},{4,5},{5,6},{6,7},{8,9},{9,10},{10,11},{11... | collective-permute-start | bytes 2359304 | tf_op jit(solution)/shard_map/ppermute | solution.py:17
  81.9 13.6 %collective-permute-start.11 = (f32[256,3,1,256]{0,3,2,1:T(8,128)}, f32[256,3,1,256]{0,3,2,1:T(8,128)}, u32[]{:S(2)}, u32[]{:S(2)}) collective-permute-start(f32[256,3,1,256]{0,3,2,1:T(8,128)} %pad_maximum_fusion.4), channel_id=1, source_target_pairs={{1,0},{2,1},{3,2},{4,3},{5,4},{6,5},{7,6},{9,8},{10,9},{11,10},{12... | collective-permute-start | bytes 2359304 | tf_op jit(solution)/shard_map/ppermute | solution.py:20
  84.0 2.0 copy-start.15
  84.0 2.0 copy-start.17
  84.8 1.2 copy-start.4
  97.2 2.2 copy-start
  207.6 0.6 copy-start.18
  308.7 7.8 %collective-permute-start.12 = (f32[256,1,1,256]{0,3,2,1:T(8,128)S(1)}, f32[256,1,1,256]{0,3,2,1:T(8,128)S(1)}, u32[]{:S(2)}, u32[]{:S(2)}) collective-permute-start(f32[256,1,1,256]{0,3,2,1:T(8,128)S(1)} %bitcast.125), channel_id=1, source_target_pairs={{0,8},{8,16},{16,24},{24,32},{32,40},{40,48},{48,56},{56,64},{64,7... | collective-permute-start | bytes 786440 | tf_op jit(solution)/shard_map/ppermute | solution.py:17
  311.6 8.8 %collective-permute-start.13 = (f32[256,1,1,256]{0,3,2,1:T(8,128)S(1)}, f32[256,1,1,256]{0,3,2,1:T(8,128)S(1)}, u32[]{:S(2)}, u32[]{:S(2)}) collective-permute-start(f32[256,1,1,256]{0,3,2,1:T(8,128)S(1)} %bitcast.126), channel_id=1, source_target_pairs={{8,0},{16,8},{24,16},{32,24},{40,32},{48,40},{56,48},{64,56},{72,6... | collective-permute-start | bytes 786440 | tf_op jit(solution)/shard_map/ppermute | solution.py:20
  320.4 13.5 %collective-permute-start.14 = (f32[256,3,1,256]{0,3,2,1:T(8,128)S(1)}, f32[256,3,1,256]{0,3,2,1:T(8,128)S(1)}, u32[]{:S(2)}, u32[]{:S(2)}) collective-permute-start(f32[256,3,1,256]{0,3,2,1:T(8,128)S(1)} %pad_maximum_fusion.5), channel_id=1, source_target_pairs={{0,1},{1,2},{2,3},{3,4},{4,5},{5,6},{6,7},{8,9},{9,10},{10,11},{11... | collective-permute-start | bytes 2359304 | tf_op jit(solution)/shard_map/ppermute | solution.py:17
  325.0 13.3 %collective-permute-start.15 = (f32[256,3,1,256]{0,3,2,1:T(8,128)S(1)}, f32[256,3,1,256]{0,3,2,1:T(8,128)S(1)}, u32[]{:S(2)}, u32[]{:S(2)}) collective-permute-start(f32[256,3,1,256]{0,3,2,1:T(8,128)S(1)} %pad_maximum_fusion.5), channel_id=1, source_target_pairs={{1,0},{2,1},{3,2},{4,3},{5,4},{6,5},{7,6},{9,8},{10,9},{11,10},{12... | collective-permute-start | bytes 2359304 | tf_op jit(solution)/shard_map/ppermute | solution.py:20
  338.5 2.2 copy-start.1
  540.9 12.6 %copy-start.7 = (f32[256,256]{0,1:T(8,128)}, f32[256,256]{0,1:T(8,128)S(1)}, u32[]{:S(2)}) copy-start(f32[256,256]{0,1:T(8,128)S(1)} %multiply_add_fusion.2) | copy-start | bytes 786436
  540.9 20.0 %copy-start.5 = (bf16[256,3,3,256]{0,3,2,1:T(8,128)(2,1)S(1)}, bf16[256,3,3,256]{0,3,2,1:T(8,128)(2,1)}, u32[]{:S(2)}) copy-start(bf16[256,3,3,256]{0,3,2,1:T(8,128)(2,1)} %copy-done.4) | copy-start | bytes 3538948
  540.9 8.8 %collective-permute-start.16 = (f32[256,1,1,256]{0,3,2,1:T(8,128)S(1)}, f32[256,1,1,256]{0,3,2,1:T(8,128)S(1)}, u32[]{:S(2)}, u32[]{:S(2)}) collective-permute-start(f32[256,1,1,256]{0,3,2,1:T(8,128)S(1)} %bitcast.134), channel_id=1, source_target_pairs={{0,8},{8,16},{16,24},{24,32},{32,40},{40,48},{48,56},{56,64},{64,7... | collective-permute-start | bytes 786440 | tf_op jit(solution)/shard_map/ppermute | solution.py:17
  544.8 8.8 %collective-permute-start.17 = (f32[256,1,1,256]{0,3,2,1:T(8,128)S(1)}, f32[256,1,1,256]{0,3,2,1:T(8,128)S(1)}, u32[]{:S(2)}, u32[]{:S(2)}) collective-permute-start(f32[256,1,1,256]{0,3,2,1:T(8,128)S(1)} %bitcast.135), channel_id=1, source_target_pairs={{8,0},{16,8},{24,16},{32,24},{40,32},{48,40},{56,48},{64,56},{72,6... | collective-permute-start | bytes 786440 | tf_op jit(solution)/shard_map/ppermute | solution.py:20
  549.7 4.9 copy-start.9
  553.5 5.5 copy-start.11
  554.6 14.1 %collective-permute-start.18 = (f32[256,3,1,256]{0,3,2,1:T(8,128)}, f32[256,3,1,256]{0,3,2,1:T(8,128)}, u32[]{:S(2)}, u32[]{:S(2)}) collective-permute-start(f32[256,3,1,256]{0,3,2,1:T(8,128)} %pad_maximum_fusion.6), channel_id=1, source_target_pairs={{0,1},{1,2},{2,3},{3,4},{4,5},{5,6},{6,7},{8,9},{9,10},{10,11},{11... | collective-permute-start | bytes 2359304 | tf_op jit(solution)/shard_map/ppermute | solution.py:17
  559.0 13.6 %collective-permute-start.19 = (f32[256,3,1,256]{0,3,2,1:T(8,128)}, f32[256,3,1,256]{0,3,2,1:T(8,128)}, u32[]{:S(2)}, u32[]{:S(2)}) collective-permute-start(f32[256,3,1,256]{0,3,2,1:T(8,128)} %pad_maximum_fusion.6), channel_id=1, source_target_pairs={{1,0},{2,1},{3,2},{4,3},{5,4},{6,5},{7,6},{9,8},{10,9},{11,10},{12... | collective-permute-start | bytes 2359304 | tf_op jit(solution)/shard_map/ppermute | solution.py:20
  565.6 7.0 copy-start.8
  565.6 7.0 copy-start.10
  565.6 7.0 copy-start.12
  574.3 1.5 copy-start.2
  578.0 104.1 %copy-start.3 = (f32[256,2304]{1,0:T(8,128)S(1)}, f32[256,2304]{1,0:T(8,128)}, u32[]{:S(2)}) copy-start(f32[256,2304]{1,0:T(8,128)} %copy.52) | copy-start | bytes 7077892
  682.1 3.0 copy-start.16
where the time goes:
time: 722 us; the launch traced here: 720 us
  blocking collectives  528 us (73%)
  starting transfers between devices  58 us (8%)
  waiting for transfers between devices  56.9 us (8%)
  local copies, waits for them, and re-layouts  43.9 us (6%)
  matrix products  22.1 us (3%)
  other arithmetic  10.7 us (1%)
    psum x5, blocking collectives, reduce_dots(): return lax.psum(columns, ('space', 'member'))  510 us
    ppermute x10, starting transfers between devices, extended(): lax.ppermute(lax.slice_in_dim(block, block.shape[dim] - width, None, axis...  30.9 us
    ppermute x10, waiting for transfers between devices, extended(): lax.ppermute(lax.slice_in_dim(block, 0, width, axis=dim), axis, backward)  24.5 us
    unnamed x48, local copies, waits for them, and re-layouts  22.1 us
    ppermute x10, waiting for transfers between devices, extended(): lax.ppermute(lax.slice_in_dim(block, block.shape[dim] - width, None, axis...  20.2 us
    all_to_all x1, blocking collectives, shards(): lax.all_to_all(increment, 'member', split_axis=0, concat_axis=2, tiled=True)  18.2 us
    ppermute x10, starting transfers between devices, extended(): lax.ppermute(lax.slice_in_dim(block, 0, width, axis=dim), axis, backward)  16.6 us
  transfers between devices with their start and end apart: 21, of which 13 were waited for; matrix products, arithmetic and copies ran while one was open for 3% of the time, Pallas kernels for 0%

commit v1 on v0

v1 whole, which is shorter than its diff:
```python
import functools
import math

import jax
import jax.numpy as jnp
from jax import lax
from jax.experimental import pallas as pl
from jax.experimental.pallas import tpu as pltpu
from jax.sharding import PartitionSpec as P

LOC = 4
NX = 4
SHIFT = 2.5
MESH = pl.DeviceIdType.MESH
F32 = jnp.float32
BF16 = jnp.bfloat16
SCALE = math.sqrt(0.5 / (LOC * LOC) * math.log2(math.e))
CUT = (9.0 * LOC * LOC - 0.5) * SCALE * SCALE
OFFSETS = [(i, j) for i in (-1, 0, 1) for j in (-1, 0, 1) if (i, j) != (0, 0)]


def slot_of(i, j):
    return (i + 1) * 3 + (j + 1)


def dot(a, b):
    return lax.dot_general(a, b, (((1,), (0,)), ((), ())), preferred_element_type=F32)


def split_dot(a, b):
    high = a.astype(BF16)
    low = (a - high.astype(F32)).astype(BF16)
    return dot(high, b) + dot(low, b)


def lanes(row):
    return jnp.transpose(jnp.broadcast_to(row, (128, row.shape[1])))


def body(
    ns,
    nm,
    prior_ref,
    meta_ref,
    noise_ref,
    out_ref,
    slab,
    part,
    slab_t,
    xp,
    meta_near,
    noise_near,
    x_near,
    pre_near,
    b_near,
    y_t,
    y_own,
    k_taper,
    k_t,
    row_l,
    col_d,
    w_t,
    v1_near,
    v2_near,
    z_all,
    out_send,
    out_recv,
    out_f,
    red_send,
    red1,
    red2,
    red3,
    total,
    aa_send,
    aa_recv,
    meta_s,
    meta_r,
    noise_s,
    noise_r,
    x_s,
    x_r,
    v1_s,
    v1_r,
    v2_s,
    v2_r,
    o_s,
    o_r,
    r1_s,
    r1_r,
    r2_s,
    r2_r,
    r3_s,
    r3_r,
    r4_s,
    r4_r,
    own_sem,
):
    s = lax.axis_index("space")
    c = lax.axis_index("member")
    nz = ns // NX
    sx = s // nz
    sz = s % nz

    def exists(i, j):
        conds = []
        if i == -1:
            conds.append(s > 0)
        if i == 1:
            conds.append(s < ns - 1)
        if j == -1:
            conds.append(c > 0)
        if j == 1:
            conds.append(c < nm - 1)
        return functools.reduce(jnp.logical_and, conds)

    def halo(src, near, send, recv, i, j):
        return pltpu.make_async_remote_copy(
            src_ref=src,
            dst_ref=near.at[slot_of(-i, -j)],
            send_sem=send.at[slot_of(i, j)],
            recv_sem=recv.at[slot_of(-i, -j)],
            device_id=(s + i, c + j),
            device_id_type=MESH,
        )

    def arrival(near, send, recv, i, j):
        return pltpu.make_async_remote_copy(
            src_ref=near.at[slot_of(i, j)],
            dst_ref=near.at[slot_of(i, j)],
            send_sem=send.at[slot_of(i, j)],
            recv_sem=recv.at[slot_of(i, j)],
            device_id=(s + i, c + j),
            device_id_type=MESH,
        )

    def halo_start(src, near, send, recv):
        for i, j in OFFSETS:
            @pl.when(exists(i, j))
            def _():
                halo(src, near, send, recv, i, j).start()

    def halo_sent(src, near, send, recv):
        for i, j in OFFSETS:
            @pl.when(exists(i, j))
            def _():
                halo(src, near, send, recv, i, j).wait_send()

    def arrive(near, send, recv, i, j):
        @pl.when(exists(i, j))
        def _():
            arrival(near, send, recv, i, j).wait_recv()

    barrier = pltpu.get_barrier_semaphore()
    count = jnp.int32(nm - 1 + NX - 1 + nz - 1)
    for d in range(1, nm):
        pl.semaphore_signal(barrier, inc=1, device_id=(s, (c + d) % nm), device_id_type=MESH)
    for i, j in OFFSETS:
        if i != 0:
            here = exists(i, j)
            count = count + here.astype(jnp.int32)

            @pl.when(here)
            def _():
                pl.semaphore_signal(barrier, inc=1, device_id=(s + i, c + j), device_id_type=MESH)
    for d in range(1, NX):
        pl.semaphore_signal(
            barrier, inc=1, device_id=(((sx + d) % NX) * nz + sz, c), device_id_type=MESH
        )
    for d in range(1, nz):
        pl.semaphore_signal(
            barrier, inc=1, device_id=(sx * nz + (sz + d) % nz, c), device_id_type=MESH
        )
    for i, j in OFFSETS:
        @pl.when(jnp.logical_not(exists(i, j)))
        def _():
            p = slot_of(i, j)
            meta_near[p] = jnp.zeros(meta_near.shape[1:], F32)
            noise_near[p] = jnp.zeros(noise_near.shape[1:], BF16)
            x_near[p] = jnp.zeros(x_near.shape[1:], BF16)
            v1_near[p] = jnp.zeros(v1_near.shape[1:], v1_near.dtype)
            v2_near[p] = jnp.zeros(v2_near.shape[1:], v2_near.dtype)
    pl.semaphore_wait(barrier, count)

    halo_start(meta_ref, meta_near, meta_s, meta_r)

    def piece(d):
        target = (c + d) % nm
        return pltpu.make_async_remote_copy(
            src_ref=prior_ref.at[:, :, pl.ds(pl.multiple_of(target * 128, 128), 128)],
            dst_ref=slab.at[pl.ds(c * 32, 32)],
            send_sem=aa_send.at[d],
            recv_sem=aa_recv.at[d],
            device_id=(s, target),
            device_id_type=MESH,
        )

    def piece_in(d):
        source = (c + nm - d) % nm
        here = slab.at[pl.ds(source * 32, 32)]
        return pltpu.make_async_remote_copy(
            src_ref=here,
            dst_ref=here,
            send_sem=aa_send.at[d],
            recv_sem=aa_recv.at[d],
            device_id=(s, (c + d) % nm),
            device_id_type=MESH,
        )

    own_piece = pltpu.make_async_copy(
        prior_ref.at[:, :, pl.ds(pl.multiple_of(c * 128, 128), 128)],
        slab.at[pl.ds(c * 32, 32)],
        own_sem,
    )
    own_piece.start()
    for d in range(1, nm):
        piece(d).start()
    halo_start(noise_ref, noise_near, noise_s, noise_r)
    meta_near[4] = meta_ref[...]
    noise_near[4] = noise_ref[...]

    for i, j in OFFSETS:
        arrive(meta_near, meta_s, meta_r, i, j)
    own_row = meta_ref[0:1, :] * SCALE
    own_col = meta_ref[1:2, :] * SCALE
    lane = lax.broadcasted_iota(jnp.int32, (256, 128), 1).astype(F32) * SCALE
    log_norm = math.log2(nm * 32 - 1)

    def taper_step(p, carry):
        m = meta_near[p]
        row_shift = ((p // 3 - 1) * 16).astype(F32)
        col_shift = ((p % 3 - 1) * 128).astype(F32)
        rl = lanes((m[0:1, :] + row_shift) * SCALE)
        cl = lanes((m[1:2, :] + col_shift) * SCALE)
        row_l[p] = rl
        gap = cl - lane
        col_d[p] = -(gap * gap) - log_norm
        for half in range(2):
            sl = slice(half * 128, half * 128 + 128)
            rg = rl - own_row[:, sl]
            cg = cl - own_col[:, sl]
            near = -(rg * rg) - (cg * cg + log_norm)
            k_taper[p, :, sl] = jnp.where(near > -CUT - log_norm, jnp.exp2(near), 0.0)
        return carry

    lax.fori_loop(0, 9, taper_step, 0)
    for i, j in OFFSETS:
        arrive(noise_near, noise_s, noise_r, i, j)

    def pre_step(p, carry):
        m = meta_near[p]
        pre_near[p] = m[3:4, :] + jnp.sqrt(m[4:5, :]) * noise_near[p].astype(F32)
        return carry

    lax.fori_loop(0, 9, pre_step, 0)

    own_r = meta_ref[0:1, :]
    own_c = meta_ref[1:2, :].astype(jnp.int32)
    row_b = jnp.broadcast_to(own_r, (32, 256))
    col_b = jnp.broadcast_to(own_c, (32, 256))
    for d in range(nm):
        if d == 0:
            own_piece.wait()
        else:
            piece_in(d).wait_recv()
        source = (c + nm - d) % nm
        base = pl.multiple_of(source * 32, 32)
        part[...] = slab[pl.ds(base, 32)].astype(F32).reshape(512, 128)
        for half in range(2):
            sl = slice(half * 128, half * 128 + 128)
            got = jnp.zeros((32, 128), F32)
            for r in range(16):
                v = part[pl.ds(r, 32, stride=16), :]
                if half == 0:
                    slab_t[r, pl.ds(base, 32), :] = v.astype(BF16)
                g = jnp.take_along_axis(v, col_b[:, sl], axis=1, mode="promise_in_bounds")
                got = jnp.where(row_b[:, sl] == float(r), g, got)
            x_near[4, pl.ds(base, 32), sl] = got.astype(BF16)
    halo_start(x_near.at[4], x_near, x_s, x_r)

    def xp_step(r, carry):
        x = slab_t[r].astype(F32)
        mean = jnp.sum(x, axis=0, keepdims=True) * (1.0 / 256.0)
        slab_t[r] = (x - mean).astype(BF16)
        return carry

    lax.fori_loop(0, 16, xp_step, 0)
    for r in range(16):
        xp[r // 2, :, (r % 2) * 128:(r % 2) * 128 + 128] = slab_t[r]

    variance = meta_ref[4:5, :]

    def near_step(p, own):
        m = meta_near[p]
        live = m[2:3, :] > 0.5
        x = x_near[p].astype(F32)
        mean = jnp.sum(x, axis=0, keepdims=True) * (1.0 / 256.0)
        y = jnp.where(live, (x - mean).astype(BF16).astype(F32), 0.0)
        b = jnp.where(live, pre_near[p] - x, 0.0)
        b_near[p] = b
        if own:
            y_own[...] = y.astype(BF16)
        yt = jnp.transpose(y).astype(BF16)
        y_t[p] = yt
        kt = (dot(yt, y_own[...]) * k_taper[p]).astype(BF16)
        k_t[p] = kt
        return split_dot(b, kt)

    acc = near_step(4, True)
    for i, j in OFFSETS:
        arrive(x_near, x_s, x_r, i, j)

    def near_loop(q, acc):
        p = q + (q >= 4).astype(jnp.int32)
        return acc + near_step(p, False)

    acc = lax.fori_loop(0, 8, near_loop, acc)
    b_own = b_near[4]
    v1 = acc + (variance - SHIFT) * b_own
    v1_near[4] = v1
    halo_start(v1_near.at[4], v1_near, v1_s, v1_r)

    def weights(low, high):
        def step(t, carry):
            g = t // 9
            p = t % 9
            cov = dot(y_t[p], xp[g])
            rl = row_l[p]
            cd = col_d[p]
            for half in range(2):
                sl = slice(half * 128, half * 128 + 128)
                gap = rl - (2 * g + half).astype(F32) * SCALE
                near = cd - gap * gap
                taper = jnp.where(near > -CUT - log_norm, jnp.exp2(near), 0.0)
                w_t[g, pl.ds(pl.multiple_of(p * 256, 256), 256), sl] = (cov[:, sl] * taper).astype(BF16)
            return carry

        lax.fori_loop(low * 9, high * 9, step, 0)

    weights(0, 3)
    for i, j in OFFSETS:
        arrive(v1_near, v1_s, v1_r, i, j)

    def apply_loop(near):
        def step(p, acc):
            return acc + split_dot(near[p], k_t[p])

        return lax.fori_loop(0, 9, step, jnp.zeros((256, 256), F32))

    v2 = apply_loop(v1_near) + (variance - SHIFT) * v1_near[4]
    v2_near[4] = v2
    halo_start(v2_near.at[4], v2_near, v2_s, v2_r)
    weights(3, 6)
    for i, j in OFFSETS:
        arrive(v2_near, v2_s, v2_r, i, j)
    last = apply_loop(v2_near) + (variance - SHIFT) * v2_near[4]

    b_own = b_near[4]
    v1 = v1_near[4]
    v2 = v2_near[4]
    ones = jnp.ones((8, 256), F32)
    for k, prod in enumerate((b_own * b_own, b_own * v1, v1 * v1, v1 * v2, v2 * v2, v2 * last)):
        row = lax.dot_general(
            ones, prod, (((1,), (1,)), ((), ())),
            precision=lax.Precision.HIGHEST, preferred_element_type=F32,
        )
        red_send[k, 0:1, :] = row[0:1, 0:128]
        red_send[k, 1:2, :] = row[0:1, 128:256]

    def reduce_copy(src, dst, send, recv, device):
        return pltpu.make_async_remote_copy(
            src_ref=src, dst_ref=dst, send_sem=send, recv_sem=recv,
            device_id=device, device_id_type=MESH,
        )

    def red1_copy(d):
        target = (c + d) % nm
        return reduce_copy(
            red_send.at[target], red1.at[d], r1_s.at[d], r1_r.at[d], (s, target)
        )

    for d in range(1, nm):
        @pl.when((c + d) % nm < 6)
        def _():
            red1_copy(d).start()
    holder = c < 6

    @pl.when(holder)
    def _():
        for d in range(1, nm):
            red1_copy(d).wait_recv()
        t = red_send[c]
        for d in range(1, nm):
            t = t + red1[d]
        red2[0] = t
        copies = [
            reduce_copy(
                red2.at[0], red2.at[d], r2_s.at[d], r2_r.at[d],
                (((sx + d) % NX) * nz + sz, c),
            )
            for d in range(1, NX)
        ]
        for copy in copies:
            copy.start()
    weights(6, 7)

    @pl.when(holder)
    def _():
        for d in range(1, NX):
            reduce_copy(
                red2.at[0], red2.at[d], r2_s.at[d], r2_r.at[d],
                (((sx + d) % NX) * nz + sz, c),
            ).wait()
        t = red2[0]
        for d in range(1, NX):
            t = t + red2[d]
        red3[0] = t
        for d in range(1, nz):
            reduce_copy(
                red3.at[0], red3.at[d], r3_s.at[d], r3_r.at[d],
                (sx * nz + (sz + d) % nz, c),
            ).start()
    weights(7, 8)

    @pl.when(holder)
    def _():
        for d in range(1, nz):
            reduce_copy(
                red3.at[0], red3.at[d], r3_s.at[d], r3_r.at[d],
                (sx * nz + (sz + d) % nz, c),
            ).wait()
        t = red3[0]
        for d in range(1, nz):
            t = t + red3[d]
        total[c] = t
        for d in range(1, nm):
            reduce_copy(
                total.at[c], total.at[c], r4_s.at[d], r4_r.at[d], (s, (c + d) % nm)
            ).start()
    for d in range(1, nm):
        source = (c + nm - d) % nm

        @pl.when(source < 6)
        def _():
            reduce_copy(
                total.at[source], total.at[source], r4_s.at[d], r4_r.at[d], (s, (c + d) % nm)
            ).wait_recv()

    mu = [total[k] for k in range(6)]

    def inner(a, b):
        terms = [x * y * mu[i + j] for i, x in enumerate(a) for j, y in enumerate(b)]
        return functools.reduce(jnp.add, terms)

    def applied(a):
        out = [SHIFT * a[0]]
        for i in range(1, len(a)):
            out.append(a[i - 1] + SHIFT * a[i])
        return out + [a[-1]]

    one = jnp.ones_like(mu[0])
    residual = [one]
    direction = [one]
    coef = []
    norm = mu[0]
    for it in range(3):
        image = applied(direction)
        step = norm / inner(direction, image)
        coef = [
            (coef[i] if i < len(coef) else 0.0) + step * x for i, x in enumerate(direction)
        ]
        if it < 2:
            padded = residual + [jnp.zeros_like(one)]
            residual = [x - step * y for x, y in zip(padded, image)]
            fresh = inner(residual, residual)
            ratio = fresh / norm
            direction = [
                x + ratio * direction[i] if i < len(direction) else x
                for i, x in enumerate(residual)
            ]
            norm = fresh

    def column(v):
        flat = jnp.concatenate([v[0:1, :], v[1:2, :]], axis=1)
        col = lanes(flat)
        return jnp.concatenate([col, col], axis=1)

    e0, e1, e2 = (column(v) for v in coef)
    for p in range(9):
        z = e0 * b_near[p] + e1 * v1_near[p] + e2 * v2_near[p]
        z_all[:, p * 256:(p + 1) * 256] = z.astype(BF16)

    def out_copy(g, d):
        target = (c + d) % nm
        return pltpu.make_async_remote_copy(
            src_ref=out_send.at[g, pl.ds(pl.multiple_of(target * 32, 32), 32)],
            dst_ref=out_recv.at[c, g],
            send_sem=o_s.at[g, d],
            recv_sem=o_r.at[g, d],
            device_id=(s, target),
            device_id_type=MESH,
        )

    for g in range(4):
        for h in range(2):
            out_send[g, :, h * 256:h * 256 + 256] = dot(z_all[...], w_t[2 * g + h]).astype(BF16)
        for d in range(1, nm):
            out_copy(g, d).start()
    for g in range(4):
        for d in range(nm):
            source = (c + nm - d) % nm
            if d == 0:
                block = out_send[g, pl.ds(pl.multiple_of(c * 32, 32), 32), :]
            else:
                there = out_recv.at[source, g]
                reduce_copy(
                    there, there, o_s.at[g, d], o_r.at[g, d], (s, (c + d) % nm)
                ).wait_recv()
                block = out_recv[source, g]
            for q in range(4):
                out_f[source, pl.ds(g * 4 + q, 32, stride=16), :] = (
                    block[:, q * 128:q * 128 + 128].astype(F32)
                )
    for k in range(nm):
        out_ref[:, :, k * 128:k * 128 + 128] = out_f[k].reshape(32, 16, 128).astype(BF16)

    halo_sent(meta_ref, meta_near, meta_s, meta_r)
    halo_sent(noise_ref, noise_near, noise_s, noise_r)
    halo_sent(x_near.at[4], x_near, x_s, x_r)
    halo_sent(v1_near.at[4], v1_near, v1_s, v1_r)
    halo_sent(v2_near.at[4], v2_near, v2_s, v2_r)
    for d in range(1, nm):
        piece(d).wait_send()

        @pl.when((c + d) % nm < 6)
        def _():
            red1_copy(d).wait_send()

        @pl.when(holder)
        def _():
            reduce_copy(
                total.at[c], total.at[c], r4_s.at[d], r4_r.at[d], (s, (c + d) % nm)
            ).wait_send()
        for g in range(4):
            out_copy(g, d).wait_send()


def shards(ns, nm, prior, location, counts, datum, draws, spread):
    obs = location.shape[1] * location.shape[2]
    cells = location.reshape(1, obs)
    slot = jnp.arange(obs, dtype=jnp.int32)[None] % location.shape[2]
    live = slot < jnp.repeat(counts.reshape(-1), location.shape[2])[None]
    meta = jnp.concatenate(
        [
            (cells // 128).astype(F32),
            (cells % 128).astype(F32),
            live.astype(F32),
            datum.reshape(1, obs),
            spread.reshape(1, obs),
            jnp.zeros((3, obs), F32),
        ]
    )
    noise = draws.reshape(draws.shape[1], obs)
    nz = ns // NX
    near = (9, 256, 256)
    dma = pltpu.SemaphoreType.DMA
    scratch = [
        pltpu.VMEM((256, 16, 128), BF16),
        pltpu.VMEM((512, 128), F32),
        pltpu.VMEM((16, 256, 128), BF16),
        pltpu.VMEM((8, 256, 256), BF16),
        pltpu.VMEM((9, 8, 256), F32),
        pltpu.VMEM(near, BF16),
        pltpu.VMEM(near, BF16),
        pltpu.VMEM(near, F32),
        pltpu.VMEM(near, F32),
        pltpu.VMEM(near, BF16),
        pltpu.VMEM((256, 256), BF16),
        pltpu.VMEM(near, F32),
        pltpu.VMEM(near, BF16),
        pltpu.VMEM((9, 256, 128), F32),
        pltpu.VMEM((9, 256, 128), F32),
        pltpu.VMEM((8, 2304, 256), BF16),
        pltpu.VMEM(near, F32),
        pltpu.VMEM(near, F32),
        pltpu.VMEM((256, 2304), BF16),
        pltpu.VMEM((4, 256, 512), BF16),
        pltpu.VMEM((8, 4, 32, 512), BF16),
        pltpu.VMEM((8, 512, 128), F32),
        pltpu.VMEM((8, 2, 128), F32),
        pltpu.VMEM((8, 2, 128), F32),
        pltpu.VMEM((NX, 2, 128), F32),
        pltpu.VMEM((nz, 2, 128), F32),
        pltpu.VMEM((8, 2, 128), F32),
        dma((8,)), dma((8,)),
        dma((9,)), dma((9,)),
        dma((9,)), dma((9,)),
        dma((9,)), dma((9,)),
        dma((9,)), dma((9,)),
        dma((9,)), dma((9,)),
        dma((4, 8)), dma((4, 8)),
        dma((8,)), dma((8,)),
        dma((NX,)), dma((NX,)),
        dma((nz,)), dma((nz,)),
        dma((8,)), dma((8,)),
        dma(()),
    ]
    return pl.pallas_call(
        functools.partial(body, ns, nm),
        out_shape=jax.ShapeDtypeStruct(prior.shape, BF16),
        in_specs=[
            pl.BlockSpec(memory_space=pl.ANY),
            pl.BlockSpec(memory_space=pltpu.VMEM),
            pl.BlockSpec(memory_space=pltpu.VMEM),
        ],
        out_specs=pl.BlockSpec(memory_space=pltpu.VMEM),
        scratch_shapes=scratch,
        compiler_params=pltpu.CompilerParams(
            collective_id=0, has_side_effects=True, vmem_limit_bytes=60 * 1024 * 1024
        ),
    )(prior, meta, noise)


def solution(mesh):
    in_specs = (
        P("member", "space", None),
        P("member", "space", None),
        P("member", "space"),
        P("member", "space", None),
        P("member", None, "space", None),
        P("member", "space", None),
    )
    out_specs = P("member", "space", None)
    return jax.shard_map(
        functools.partial(shards, mesh.shape["space"], mesh.shape["member"]),
        mesh=mesh, in_specs=in_specs, out_specs=out_specs, check_vma=False,
    )
```

time: 722 us -> 140 us (0.19)
  blocking collectives: 528 us -> 0 us
  Pallas kernels: 0 us -> 133 us
  starting transfers between devices: 58 us -> 0 us
  waiting for transfers between devices: 56.9 us -> 0 us
  local copies, waits for them, and re-layouts: 43.9 us -> 6.56 us
  matrix products: 22.1 us -> 0 us
  other arithmetic: 10.7 us -> 0.03 us
    psum x5 -> x0, blocking collectives: 510 us -> none  [reduce_dots(): return lax.psum(columns, ('space', 'member'))]
    pallas_call x0 -> x1, Pallas kernels: none -> 133 us  [shards(): pl.pallas_call(functools.partial(body, ns, nm), out_shape=jax.ShapeDtypeS...]
    ppermute x20 -> x0, starting transfers between devices: 47.6 us -> none  [the longest x10 30.9 us: extended(): lax.ppermute(lax.slice_in_dim(block, block.shape[dim] - width, None, axis...]
    ppermute x20 -> x0, waiting for transfers between devices: 44.7 us -> none  [the longest x10 24.5 us: extended(): lax.ppermute(lax.slice_in_dim(block, 0, width, axis=dim), axis, backward)]
    dot_general x8 -> x0, matrix products: 22.1 us -> none  [the longest x4 14.3 us: add_block(): lax.dot_general(weights_z, weight_tile, (((1,), (1,)), ((), ())), preferr...]
    all_to_all x1 -> x0, blocking collectives: 18.2 us -> none  [shards(): lax.all_to_all(increment, 'member', split_axis=0, concat_axis=2, tiled=True)]
    unnamed x48 -> x10, local copies, waits for them, and re-layouts: 22.1 us -> 5.88 us
    all_to_all x1 -> x0, waiting for transfers between devices: 12.2 us -> none  [shards(): lax.all_to_all(prior_ensemble, 'member', split_axis=2, concat_axis=0, til...]
  transfers between devices with their start and end apart: 21 -> 0, of which waited for: 13 -> 0; matrix products, arithmetic and copies ran while one was open for 3% -> 0% of each run, Pallas kernels for 0% -> 0%
where the time goes in v1:
time: 140 us
  Pallas kernels  133 us (95%)
  local copies, waits for them, and re-layouts  6.56 us (5%)
    pallas_call x1, Pallas kernels, shards(): pl.pallas_call(functools.partial(body, ns, nm), out_shape=jax.ShapeDtypeS...  133 us
    unnamed x10, local copies, waits for them, and re-layouts  5.88 us

profile of v1, /device:TPU:1, one launch (start us, length us, event | category | flops | bytes accessed | tf_op | source)
XLA Modules:
  0.0 139.6 jit_solution(16644567956417580213)
XLA Ops:
  0.0 0.0 copy-start.3
  0.0 0.7 copy-done.3
  0.7 0.1 broadcast_in_dim.7
  0.7 0.0 copy-start
  0.7 0.7 copy-done
  1.4 0.0 copy-start.1
  1.4 0.0 copy-start.2
  1.5 0.6 copy-done.1
  2.1 0.0 copy-done.2
  2.1 0.6 concatenate.3.meta_ref
  2.7 1.6 %copy.9 = bf16[32,8,2,128]{3,1,2,0:T(8,128)(2,1)} copy(bf16[32,8,2,128]{3,2,1,0:T(2,128)(2,1)} %bitcast.11) | data formatting | bytes 262144
  4.3 133.0 %shard_map.64 = bf16[32,16,1024]{2,1,0:T(8,128)(2,1)} custom-call(bf16[32,16,1024]{2,1,0:T(8,128)(2,1)} %prior_ref.1, f32[8,256]{1,0:T(8,128)} %concatenate.3.meta_ref, bf16[256,256]{1,0:T(8,128)(2,1)} %bitcast.10), custom_call_target="tpu_custom_call" | custom-call | tf_op jit(solution)/shard_map/pallas_call | solution.py:607
  137.3 2.3 %copy.11 = bf16[32,16,1024]{2,1,0:T(8,128)(2,1)} copy(bf16[32,16,1024]{2,1,0:T(8,128)(2,1)} %shard_map.64) | data formatting | bytes 2097152
  (4 shorter events, 0.0 us)
Async XLA Ops:
  0.0 0.7 copy-start.3
  0.7 0.7 copy-start
  1.4 0.7 copy-start.1
  1.4 0.7 copy-start.2

commit v2 on v1

v2 whole, which is shorter than its diff:
```python
import functools
import math

import jax
import jax.numpy as jnp
from jax import lax
from jax.experimental import pallas as pl
from jax.experimental.pallas import tpu as pltpu
from jax.sharding import PartitionSpec as P

LOC = 4
NX = 4
SHIFT = 2.5
MESH = pl.DeviceIdType.MESH
F32 = jnp.float32
BF16 = jnp.bfloat16
SCALE = math.sqrt(0.5 / (LOC * LOC) * math.log2(math.e))
CUT = (9.0 * LOC * LOC - 0.5) * SCALE * SCALE
OFFSETS = [(i, j) for i in (-1, 0, 1) for j in (-1, 0, 1) if (i, j) != (0, 0)]


def slot_of(i, j):
    return (i + 1) * 3 + (j + 1)


def dot(a, b):
    return lax.dot_general(a, b, (((1,), (0,)), ((), ())), preferred_element_type=F32)


def split_dot(a, b):
    high = a.astype(BF16)
    low = (a - high.astype(F32)).astype(BF16)
    return dot(high, b) + dot(low, b)


def lanes(row):
    return jnp.transpose(jnp.broadcast_to(row, (128, row.shape[1])))


def body(
    ns,
    nm,
    prior_ref,
    meta_ref,
    noise_ref,
    out_ref,
    slab,
    packed,
    part,
    slab_t,
    xp,
    meta_near,
    noise_near,
    x_near,
    pre_near,
    b_near,
    y_t,
    y_own,
    k_taper,
    k_t,
    row_l,
    col_d,
    w_t,
    v1_near,
    v2_near,
    v1_low,
    v2_low,
    v1_own,
    v2_own,
    z_all,
    out_send,
    out_recv,
    out_f,
    early,
    early1,
    early2,
    early3,
    late,
    late1,
    late2,
    late3,
    aa_send,
    aa_recv,
    meta_s,
    meta_r,
    noise_s,
    noise_r,
    x_s,
    x_r,
    v1_s,
    v1_r,
    v2_s,
    v2_r,
    v1_ls,
    v1_lr,
    v2_ls,
    v2_lr,
    o_s,
    o_r,
    r1_s,
    r1_r,
    r2_s,
    r2_r,
    r3_s,
    r3_r,
    e1_s,
    e1_r,
    e2_s,
    e2_r,
    e3_s,
    e3_r,
    own_sem,
    pack_sem,
):
    s = lax.axis_index("space")
    c = lax.axis_index("member")
    nz = ns // NX
    sx = s // nz
    sz = s % nz

    def exists(i, j):
        conds = []
        if i == -1:
            conds.append(s > 0)
        if i == 1:
            conds.append(s < ns - 1)
        if j == -1:
            conds.append(c > 0)
        if j == 1:
            conds.append(c < nm - 1)
        return functools.reduce(jnp.logical_and, conds)

    ends = []


    def remote(src, dst, send, recv, device):
        return pltpu.make_async_remote_copy(
            src_ref=src, dst_ref=dst, send_sem=send, recv_sem=recv,
            device_id=device, device_id_type=MESH,
        )

    def send_if(cond, make):
        if cond is True:
            make().start()
            ends.append(lambda: make().wait_send())
            return

        @pl.when(cond)
        def _():
            make().start()

        def finish():
            @pl.when(cond)
            def _():
                make().wait_send()

        ends.append(finish)

    def halo(src, near, send, recv, i, j, h):
        rows = pl.ds(h * (src.shape[0] // recv.shape[1]), src.shape[0] // recv.shape[1])
        send_if(exists(i, j), lambda: remote(
            src.at[rows], near.at[slot_of(-i, -j), rows],
            send.at[slot_of(i, j), h], recv.at[slot_of(-i, -j), h], (s + i, c + j),
        ))

    def start(near, send, recv, src=None):
        src = near.at[4] if src is None else src
        for h in range(recv.shape[1]):
            for i, j in ((-1, 0), (1, 0), (0, -1), (0, 1)):
                halo(src, near, send, recv, i, j, h)

    def landed(near, send, recv, i, j, h):
        count = near.shape[1] // recv.shape[1]
        there = near.at[slot_of(i, j), pl.ds(h * count, count)]

        @pl.when(exists(i, j))
        def _():
            remote(
                there, there, send.at[slot_of(i, j), h], recv.at[slot_of(i, j), h],
                (s + i, c + j),
            ).wait_recv()

    def forward(near, send, recv, h):
        count = near.shape[1] // recv.shape[1]
        rows = pl.ds(h * count, count)
        for i in (-1, 1):
            landed(near, send, recv, i, 0, h)
            for j in (-1, 1):
                send_if(
                    jnp.logical_and(exists(i, 0), exists(0, j)),
                    functools.partial(
                        remote, near.at[slot_of(i, 0), rows], near.at[slot_of(i, -j), rows],
                        send.at[slot_of(i, j), h], recv.at[slot_of(i, -j), h], (s, c + j),
                    ),
                )

    def settle(near, send, recv):
        for h in range(recv.shape[1]):
            for i, j in ((0, -1), (0, 1), (-1, -1), (-1, 1), (1, -1), (1, 1)):
                landed(near, send, recv, i, j, h)

    def low_copy(low, send, recv, i):
        return remote(
            low.at[1], low.at[1 - i], send.at[1 + i], recv.at[1 - i], (s + i, c)
        )

    def start_low(low, send, recv):
        for i in (-1, 1):
            send_if(exists(i, 0), functools.partial(low_copy, low, send, recv, i))

    def settle_low(low, send, recv):
        for i in (-1, 1):
            @pl.when(exists(i, 0))
            def _():
                remote(
                    low.at[1 + i], low.at[1 + i], send.at[1 + i], recv.at[1 + i], (s + i, c)
                ).wait_recv()

    def pack(d):
        target = (c + d) % nm
        return pltpu.make_async_copy(
            prior_ref.at[:, :, pl.ds(pl.multiple_of(target * 128, 128), 128)],
            packed.at[d], pack_sem.at[d],
        )

    for d in range(1, nm):
        pack(d).start()
    own_piece = pltpu.make_async_copy(
        prior_ref.at[:, :, pl.ds(pl.multiple_of(c * 128, 128), 128)],
        slab.at[pl.ds(c * 32, 32)],
        own_sem,
    )
    own_piece.start()
    barrier = pltpu.get_barrier_semaphore()
    count = jnp.int32(nm - 1 + NX - 1 + nz - 1)
    for d in range(1, nm):
        pl.semaphore_signal(barrier, inc=1, device_id=(s, (c + d) % nm), device_id_type=MESH)
    for i in (-1, 1):
        here = exists(i, 0)
        count = count + here.astype(jnp.int32)

        @pl.when(here)
        def _():
            pl.semaphore_signal(barrier, inc=1, device_id=(s + i, c), device_id_type=MESH)
    for d in range(1, NX):
        pl.semaphore_signal(
            barrier, inc=1, device_id=(((sx + d) % NX) * nz + sz, c), device_id_type=MESH
        )
    for d in range(1, nz):
        pl.semaphore_signal(
            barrier, inc=1, device_id=(sx * nz + (sz + d) % nz, c), device_id_type=MESH
        )
    for i, j in OFFSETS:
        @pl.when(jnp.logical_not(exists(i, j)))
        def _():
            p = slot_of(i, j)
            meta_near[p] = jnp.zeros(meta_near.shape[1:], F32)
            noise_near[p] = jnp.zeros(noise_near.shape[1:], BF16)
            x_near[p] = jnp.zeros(x_near.shape[1:], BF16)
            v1_near[p] = jnp.zeros(v1_near.shape[1:], BF16)
            v2_near[p] = jnp.zeros(v2_near.shape[1:], BF16)
            if j == 0:
                v1_low[1 + i] = jnp.zeros(v1_low.shape[1:], BF16)
                v2_low[1 + i] = jnp.zeros(v2_low.shape[1:], BF16)
    for d in range(1, nm):
        pack(d).wait()
    pl.semaphore_wait(barrier, count)

    meta_near[4] = meta_ref[...]
    noise_near[4] = noise_ref[...]
    start(meta_near, meta_s, meta_r)
    for d in range(1, nm):
        target = (c + d) % nm
        send_if(d > 0, functools.partial(
            remote,
            packed.at[d], slab.at[pl.ds(c * 32, 32)], aa_send.at[d], aa_recv.at[d], (s, target),
        ))
    for j in (-1, 1):
        halo(noise_near.at[4], noise_near, noise_s, noise_r, 0, j, 0)
    for i in (-1, 1):
        halo(noise_near.at[4], noise_near, noise_s, noise_r, i, 0, 0)
    forward(meta_near, meta_s, meta_r, 0)
    mate = 1 - 2 * (c % 2)
    outer = -mate
    has_outer = jnp.logical_and(c + outer >= 0, c + outer < nm)

    def noise_landed(cond, i, j):
        there = noise_near.at[slot_of(i, j)]

        @pl.when(cond)
        def _():
            remote(
                there, there, noise_s.at[slot_of(i, j), 0], noise_r.at[slot_of(i, j), 0],
                (s, c + mate),
            ).wait_recv()

    def noise_second():
        noise_landed(has_outer, 0, outer)
        for i in (-1, 1):
            send_if(jnp.logical_and(exists(i, 0), has_outer), functools.partial(
                remote, noise_near.at[slot_of(0, outer)], noise_near.at[slot_of(-i, outer)],
                noise_s.at[slot_of(i, -1), 0], noise_r.at[slot_of(-i, outer), 0], (s + i, c),
            ))

    def noise_third():
        for i in (-1, 1):
            noise_landed(exists(i, 0), i, 0)
            send_if(exists(i, 0), functools.partial(
                remote, noise_near.at[slot_of(i, 0)], noise_near.at[slot_of(i, -mate)],
                noise_s.at[slot_of(i, 1), 0], noise_r.at[slot_of(i, -mate), 0], (s, c + mate),
            ))

    def noise_settle():
        noise_landed(c >= 0, 0, mate)
        for i in (-1, 1):
            noise_landed(exists(i, 0), i, mate)
            noise_landed(jnp.logical_and(exists(i, 0), has_outer), i, outer)

    def piece_wait(d):
        here = slab.at[pl.ds(((c + nm - d) % nm) * 32, 32)]
        remote(here, here, aa_send.at[d], aa_recv.at[d], (s, (c + d) % nm)).wait_recv()

    settle(meta_near, meta_s, meta_r)
    own_row = meta_ref[0:1, :] * SCALE
    own_col = meta_ref[1:2, :] * SCALE
    lane = lax.broadcasted_iota(jnp.int32, (256, 128), 1).astype(F32) * SCALE
    log_norm = math.log2(nm * 32 - 1)

    def taper_step(p, carry):
        m = meta_near[p]
        row_shift = ((p // 3 - 1) * 16).astype(F32)
        col_shift = ((p % 3 - 1) * 128).astype(F32)
        rl = lanes((m[0:1, :] + row_shift) * SCALE)
        cl = lanes((m[1:2, :] + col_shift) * SCALE)
        row_l[p] = rl
        gap = cl - lane
        col_d[p] = -(gap * gap) - log_norm
        for half in range(2):
            sl = slice(half * 128, half * 128 + 128)
            rg = rl - own_row[:, sl]
            cg = cl - own_col[:, sl]
            near = -(rg * rg) - (cg * cg + log_norm)
            k_taper[p, :, sl] = jnp.where(near > -CUT - log_norm, jnp.exp2(near), 0.0)
        return carry

    lax.fori_loop(0, 9, taper_step, 0)
    noise_second()
    noise_third()
    noise_settle()

    def pre_step(p, carry):
        m = meta_near[p]
        pre_near[p] = m[3:4, :] + jnp.sqrt(m[4:5, :]) * noise_near[p].astype(F32)
        return carry

    lax.fori_loop(0, 9, pre_step, 0)

    own_r = meta_ref[0:1, :]
    own_c = meta_ref[1:2, :].astype(jnp.int32)
    row_b = jnp.broadcast_to(own_r, (32, 256))
    col_b = jnp.broadcast_to(own_c, (32, 256))
    for d in range(nm):
        if d == 0:
            own_piece.wait()
        else:
            piece_wait(d)
        source = (c + nm - d) % nm
        base = pl.multiple_of(source * 32, 32)
        part[...] = slab[pl.ds(base, 32)].astype(F32).reshape(512, 128)
        for half in range(2):
            sl = slice(half * 128, half * 128 + 128)
            got = jnp.zeros((32, 128), F32)
            for r in range(16):
                v = part[pl.ds(r, 32, stride=16), :]
                if half == 0:
                    slab_t[r, pl.ds(base, 32), :] = v.astype(BF16)
                g = jnp.take_along_axis(v, col_b[:, sl], axis=1, mode="promise_in_bounds")
                got = jnp.where(row_b[:, sl] == float(r), g, got)
            x_near[4, pl.ds(base, 32), sl] = got.astype(BF16)
    start(x_near, x_s, x_r)

    def xp_step(r, carry):
        x = slab_t[r].astype(F32)
        mean = jnp.sum(x, axis=0, keepdims=True) * (1.0 / 256.0)
        slab_t[r] = (x - mean).astype(BF16)
        return carry

    lax.fori_loop(0, 8, xp_step, 0)
    forward(x_near, x_s, x_r, 0)
    lax.fori_loop(8, 16, xp_step, 0)
    forward(x_near, x_s, x_r, 1)
    for r in range(16):
        xp[r // 2, :, (r % 2) * 128:(r % 2) * 128 + 128] = slab_t[r]

    variance = meta_ref[4:5, :]

    def near_step(p, own):
        m = meta_near[p]
        live = m[2:3, :] > 0.5
        x = x_near[p].astype(F32)
        mean = jnp.sum(x, axis=0, keepdims=True) * (1.0 / 256.0)
        y = jnp.where(live, (x - mean).astype(BF16).astype(F32), 0.0)
        b = jnp.where(live, pre_near[p] - x, 0.0)
        b_near[p] = b
        if own:
            y_own[...] = y.astype(BF16)
        yt = jnp.transpose(y).astype(BF16)
        y_t[p] = yt
        kt = (dot(yt, y_own[...]) * k_taper[p]).astype(BF16)
        k_t[p] = kt
        if own:
            return split_dot(b, kt)
        return dot(b.astype(BF16), kt)

    acc = near_step(4, True)
    settle(x_near, x_s, x_r)

    def near_loop(q, acc):
        p = q + (q >= 4).astype(jnp.int32)
        return acc + near_step(p, False)

    acc = lax.fori_loop(0, 8, near_loop, acc)
    b_own = b_near[4]
    v1 = acc + (variance - SHIFT) * b_own

    def share(v, near, low, send, recv):
        high = v.astype(BF16)
        near[4] = high
        start(near, send, recv)
        low[1] = (v - high.astype(F32)).astype(BF16)

    share(v1, v1_near, v1_low, v1_s, v1_r)

    def weights(low, high):
        def step(t, carry):
            g = t // 9
            p = t % 9
            cov = dot(y_t[p], xp[g])
            rl = row_l[p]
            cd = col_d[p]
            for half in range(2):
                sl = slice(half * 128, half * 128 + 128)
                gap = rl - (2 * g + half).astype(F32) * SCALE
                near = cd - gap * gap
                taper = jnp.where(near > -CUT - log_norm, jnp.exp2(near), 0.0)
                w_t[g, pl.ds(pl.multiple_of(p * 256, 256), 256), sl] = (cov[:, sl] * taper).astype(BF16)
            return carry

        lax.fori_loop(low * 9, high * 9, step, 0)

    v1_own[...] = v1
    weights(0, 1)
    forward(v1_near, v1_s, v1_r, 0)
    start_low(v1_low, v1_ls, v1_lr)
    weights(1, 2)
    forward(v1_near, v1_s, v1_r, 1)
    weights(2, 3)
    settle_low(v1_low, v1_ls, v1_lr)
    settle(v1_near, v1_s, v1_r)

    def apply_near(near, low):
        def step(p, acc):
            return acc + dot(near[p], k_t[p])

        acc = lax.fori_loop(0, 9, step, jnp.zeros((256, 256), F32))
        for i in range(3):
            acc = acc + dot(low[i], k_t[3 * i + 1])
        return acc

    v2 = apply_near(v1_near, v1_low) + (variance - SHIFT) * v1_own[...]
    share(v2, v2_near, v2_low, v2_s, v2_r)
    v2_own[...] = v2
    members = [(s, (c + d) % nm) for d in range(1, nm)]
    along_x = [(((sx + d) % NX) * nz + sz, c) for d in range(1, NX)]
    along_z = [(sx * nz + (sz + d) % nz, c) for d in range(1, nz)]

    def spread(source, into, send, recv, devices):
        for k, device in enumerate(devices):
            send_if(True, functools.partial(
                remote, source, into.at[k], send.at[k], recv.at[k], device
            ))

    def collect(own, into, send, recv, devices):
        for k, device in enumerate(devices):
            remote(into.at[k], into.at[k], send.at[k], recv.at[k], device).wait_recv()
        for k in range(len(devices)):
            own = own + into[k]
        return own

    def total_row(ref, k, prod):
        half = prod[:, 0:128] + prod[:, 128:256]
        row = jnp.sum(jnp.transpose(half), axis=0, keepdims=True)
        ref[k:k + 1, :] = row[:, 0:128]
        ref[k + 1:k + 2, :] = row[:, 128:256]

    b_own = b_near[4]
    v1 = v1_own[...]
    v2 = v2_own[...]
    early[0] = jnp.zeros(early.shape[1:], F32)
    for k, prod in enumerate((b_own * b_own, b_own * v1, v1 * v1, v1 * v2, v2 * v2)):
        total_row(early.at[0], 2 * k, prod)
    weights(3, 4)
    forward(v2_near, v2_s, v2_r, 0)
    start_low(v2_low, v2_ls, v2_lr)
    spread(early.at[0], early1, e1_s, e1_r, members)
    weights(4, 5)
    forward(v2_near, v2_s, v2_r, 1)
    weights(5, 6)
    early[1] = collect(early[0], early1, e1_s, e1_r, members)
    spread(early.at[1], early2, e2_s, e2_r, along_x)
    settle_low(v2_low, v2_ls, v2_lr)
    settle(v2_near, v2_s, v2_r)
    v2 = v2_own[...]
    total_row(late.at[0], 0, v2 * (apply_near(v2_near, v2_low) + (variance - SHIFT) * v2))
    spread(late.at[0], late1, r1_s, r1_r, members)
    early[2] = collect(early[1], early2, e2_s, e2_r, along_x)
    spread(early.at[2], early3, e3_s, e3_r, along_z)
    weights(6, 7)
    late[1] = collect(late[0], late1, r1_s, r1_r, members)
    spread(late.at[1], late2, r2_s, r2_r, along_x)
    weights(7, 8)
    late[2] = collect(late[1], late2, r2_s, r2_r, along_x)
    spread(late.at[2], late3, r3_s, r3_r, along_z)
    first = collect(early[2], early3, e3_s, e3_r, along_z)
    final = collect(late[2], late3, r3_s, r3_r, along_z)

    mu = [first[2 * k:2 * k + 2] for k in range(5)] + [final]

    def inner(a, b):
        terms = [x * y * mu[i + j] for i, x in enumerate(a) for j, y in enumerate(b)]
        return functools.reduce(jnp.add, terms)

    def applied(a):
        out = [SHIFT * a[0]]
        for i in range(1, len(a)):
            out.append(a[i - 1] + SHIFT * a[i])
        return out + [a[-1]]

    one = jnp.ones_like(mu[0])
    residual = [one]
    direction = [one]
    coef = []
    norm = mu[0]
    for it in range(3):
        image = applied(direction)
        step = norm / inner(direction, image)
        coef = [
            (coef[i] if i < len(coef) else 0.0) + step * x for i, x in enumerate(direction)
        ]
        if it < 2:
            padded = residual + [jnp.zeros_like(one)]
            residual = [x - step * y for x, y in zip(padded, image)]
            fresh = inner(residual, residual)
            ratio = fresh / norm
            direction = [
                x + ratio * direction[i] if i < len(direction) else x
                for i, x in enumerate(residual)
            ]
            norm = fresh

    def column(v):
        flat = jnp.concatenate([v[0:1, :], v[1:2, :]], axis=1)
        col = lanes(flat)
        return jnp.concatenate([col, col], axis=1)

    e0, e1, e2 = (column(v) for v in coef)
    for p in range(9):
        first = v1_near[p].astype(F32)
        second = v2_near[p].astype(F32)
        if p % 3 == 1:
            first = first + v1_low[p // 3].astype(F32)
            second = second + v2_low[p // 3].astype(F32)
        z = e0 * b_near[p] + e1 * first + e2 * second
        z_all[:, p * 256:(p + 1) * 256] = z.astype(BF16)


    def out_copy(g, d):
        target = (c + d) % nm
        return remote(
            out_send.at[g, pl.ds(pl.multiple_of(target * 32, 32), 32)], out_recv.at[c, g],
            o_s.at[g, d], o_r.at[g, d], (s, target),
        )

    for g in range(4):
        for h in range(2):
            out_send[g, :, h * 256:h * 256 + 256] = dot(z_all[...], w_t[2 * g + h]).astype(BF16)
        for d in range(1, nm):
            send_if(d > 0, functools.partial(out_copy, g, d))
    for g in range(4):
        for d in range(nm):
            source = (c + nm - d) % nm
            if d == 0:
                block = out_send[g, pl.ds(pl.multiple_of(c * 32, 32), 32), :]
            else:
                there = out_recv.at[source, g]
                remote(
                    there, there, o_s.at[g, d], o_r.at[g, d], (s, (c + d) % nm)
                ).wait_recv()
                block = out_recv[source, g]
            for q in range(4):
                out_f[source, pl.ds(g * 4 + q, 32, stride=16), :] = (
                    block[:, q * 128:q * 128 + 128].astype(F32)
                )
    for k in range(nm):
        out_ref[:, :, k * 128:k * 128 + 128] = out_f[k].reshape(32, 16, 128).astype(BF16)

    for finish in ends:
        finish()


def shards(ns, nm, prior, location, counts, datum, draws, spread):
    obs = location.shape[1] * location.shape[2]
    cells = location.reshape(1, obs)
    slot = jnp.arange(obs, dtype=jnp.int32)[None] % location.shape[2]
    live = slot < jnp.repeat(counts.reshape(-1), location.shape[2])[None]
    meta = jnp.concatenate(
        [
            (cells // 128).astype(F32),
            (cells % 128).astype(F32),
            live.astype(F32),
            datum.reshape(1, obs),
            spread.reshape(1, obs),
            jnp.zeros((3, obs), F32),
        ]
    )
    noise = draws.reshape(draws.shape[1], obs)
    nz = ns // NX
    near = (9, 256, 256)
    dma = pltpu.SemaphoreType.DMA
    scratch = [
        pltpu.VMEM((256, 16, 128), BF16),
        pltpu.VMEM((8, 32, 16, 128), BF16),
        pltpu.VMEM((512, 128), F32),
        pltpu.VMEM((16, 256, 128), BF16),
        pltpu.VMEM((8, 256, 256), BF16),
        pltpu.VMEM((9, 8, 256), F32),
        pltpu.VMEM(near, BF16),
        pltpu.VMEM(near, BF16),
        pltpu.VMEM(near, F32),
        pltpu.VMEM(near, F32),
        pltpu.VMEM(near, BF16),
        pltpu.VMEM((256, 256), BF16),
        pltpu.VMEM(near, F32),
        pltpu.VMEM(near, BF16),
        pltpu.VMEM((9, 256, 128), F32),
        pltpu.VMEM((9, 256, 128), F32),
        pltpu.VMEM((8, 2304, 256), BF16),
        pltpu.VMEM(near, BF16),
        pltpu.VMEM(near, BF16),
        pltpu.VMEM((3, 256, 256), BF16),
        pltpu.VMEM((3, 256, 256), BF16),
        pltpu.VMEM((256, 256), F32),
        pltpu.VMEM((256, 256), F32),
        pltpu.VMEM((256, 2304), BF16),
        pltpu.VMEM((4, 256, 512), BF16),
        pltpu.VMEM((8, 4, 32, 512), BF16),
        pltpu.VMEM((8, 512, 128), F32),
        pltpu.VMEM((3, 16, 128), F32),
        pltpu.VMEM((7, 16, 128), F32),
        pltpu.VMEM((NX - 1, 16, 128), F32),
        pltpu.VMEM((nz - 1, 16, 128), F32),
        pltpu.VMEM((3, 2, 128), F32),
        pltpu.VMEM((7, 2, 128), F32),
        pltpu.VMEM((NX - 1, 2, 128), F32),
        pltpu.VMEM((nz - 1, 2, 128), F32),
        dma((8,)), dma((8,)),
        dma((9, 1)), dma((9, 1)),
        dma((9, 1)), dma((9, 1)),
        dma((9, 2)), dma((9, 2)),
        dma((9, 2)), dma((9, 2)),
        dma((9, 2)), dma((9, 2)),
        dma((3,)), dma((3,)),
        dma((3,)), dma((3,)),
        dma((4, 8)), dma((4, 8)),
        dma((8,)), dma((8,)),
        dma((NX,)), dma((NX,)),
        dma((nz,)), dma((nz,)),
        dma((8,)), dma((8,)),
        dma((NX,)), dma((NX,)),
        dma((nz,)), dma((nz,)),
        dma(()),
        dma((8,)),
    ]
    return pl.pallas_call(
        functools.partial(body, ns, nm),
        out_shape=jax.ShapeDtypeStruct(prior.shape, BF16),
        in_specs=[
            pl.BlockSpec(memory_space=pl.ANY),
            pl.BlockSpec(memory_space=pltpu.VMEM),
            pl.BlockSpec(memory_space=pltpu.VMEM),
        ],
        out_specs=pl.BlockSpec(memory_space=pltpu.VMEM),
        scratch_shapes=scratch,
        compiler_params=pltpu.CompilerParams(
            collective_id=0, has_side_effects=True, vmem_limit_bytes=60 * 1024 * 1024
        ),
    )(prior, meta, noise)


def solution(mesh):
    in_specs = (
        P("member", "space", None),
        P("member", "space", None),
        P("member", "space"),
        P("member", "space", None),
        P("member", None, "space", None),
        P("member", "space", None),
    )
    out_specs = P("member", "space", None)
    return jax.shard_map(
        functools.partial(shards, mesh.shape["space"], mesh.shape["member"]),
        mesh=mesh, in_specs=in_specs, out_specs=out_specs, check_vma=False,
    )
```

time: 140 us -> 116 us (0.83)
  Pallas kernels: 133 us -> 109 us
    pallas_call x1, Pallas kernels: 133 us -> 109 us  [shards(): pl.pallas_call(functools.partial(body, ns, nm), out_shape=jax.ShapeDtypeS...]
where the time goes in v2:
time: 116 us
  Pallas kernels  109 us (94%)
  local copies, waits for them, and re-layouts  6.56 us (6%)
    pallas_call x1, Pallas kernels, shards(): pl.pallas_call(functools.partial(body, ns, nm), out_shape=jax.ShapeDtypeS...  109 us
    unnamed x10, local copies, waits for them, and re-layouts  5.88 us

profile of v2, /device:TPU:1, one launch (start us, length us, event | category | flops | bytes accessed | tf_op | source)
XLA Modules:
  0.0 115.9 jit_solution(5869912754878783178)
XLA Ops:
  0.0 0.0 copy-start.3
  0.0 0.7 copy-done.3
  0.7 0.1 broadcast_in_dim.7
  0.7 0.0 copy-start
  0.7 0.7 copy-done
  1.4 0.0 copy-start.1
  1.4 0.0 copy-start.2
  1.5 0.6 copy-done.1
  2.1 0.0 copy-done.2
  2.1 0.6 concatenate.3.meta_ref
  2.7 1.6 %copy.9 = bf16[32,8,2,128]{3,1,2,0:T(8,128)(2,1)} copy(bf16[32,8,2,128]{3,2,1,0:T(2,128)(2,1)} %bitcast.11) | data formatting | bytes 262144
  4.3 109.3 %shard_map.64 = bf16[32,16,1024]{2,1,0:T(8,128)(2,1)} custom-call(bf16[32,16,1024]{2,1,0:T(8,128)(2,1)} %prior_ref.1, f32[8,256]{1,0:T(8,128)} %concatenate.3.meta_ref, bf16[256,256]{1,0:T(8,128)(2,1)} %bitcast.10), custom_call_target="tpu_custom_call" | custom-call | tf_op jit(solution)/shard_map/pallas_call | solution.py:684
  113.6 2.3 %copy.11 = bf16[32,16,1024]{2,1,0:T(8,128)(2,1)} copy(bf16[32,16,1024]{2,1,0:T(8,128)(2,1)} %shard_map.64) | data formatting | bytes 2097152
  (4 shorter events, 0.0 us)
Async XLA Ops:
  0.0 0.7 copy-start.3
  0.7 0.7 copy-start
  1.4 0.7 copy-start.1
  1.4 0.7 copy-start.2

commit v3 on v2

--- a/solution.py
+++ b/solution.py
@@ -41,7 +41,10 @@
     ns,
     nm,
     prior_ref,
-    meta_ref,
+    location_ref,
+    count_ref,
+    datum_ref,
+    spread_ref,
     noise_ref,
     out_ref,
     slab,
@@ -52,7 +55,6 @@
     meta_near,
     noise_near,
     x_near,
-    pre_near,
     b_near,
     y_t,
     y_own,
@@ -266,19 +268,32 @@
         pack(d).wait()
     pl.semaphore_wait(barrier, count)
 
-    meta_near[4] = meta_ref[...]
+    def flat(ref):
+        return jnp.concatenate([ref[0, 0:1, :], ref[0, 1:2, :]], axis=1)
+
+    cells = flat(location_ref)
+    slot = lax.broadcasted_iota(jnp.int32, (1, 128), 1)
+    live = jnp.concatenate(
+        [jnp.where(slot < count_ref[0, k], 1.0, 0.0) for k in range(2)], axis=1
+    )
+    meta_near[4, 0:1, :] = lax.shift_right_arithmetic(cells, 7).astype(F32)
+    meta_near[4, 1:2, :] = lax.bitwise_and(cells, 127).astype(F32)
+    meta_near[4, 2:3, :] = live
+    meta_near[4, 3:4, :] = flat(datum_ref)
+    meta_near[4, 4:5, :] = flat(spread_ref)
+    meta_near[4, 5:8, :] = jnp.zeros((3, 256), F32)
     noise_near[4] = noise_ref[...]
     start(meta_near, meta_s, meta_r)
+    for j in (-1, 1):
+        halo(noise_near.at[4], noise_near, noise_s, noise_r, 0, j, 0)
+    for i in (-1, 1):
+        halo(noise_near.at[4], noise_near, noise_s, noise_r, i, 0, 0)
     for d in range(1, nm):
         target = (c + d) % nm
         send_if(d > 0, functools.partial(
             remote,
             packed.at[d], slab.at[pl.ds(c * 32, 32)], aa_send.at[d], aa_recv.at[d], (s, target),
         ))
-    for j in (-1, 1):
-        halo(noise_near.at[4], noise_near, noise_s, noise_r, 0, j, 0)
-    for i in (-1, 1):
-        halo(noise_near.at[4], noise_near, noise_s, noise_r, i, 0, 0)
     forward(meta_near, meta_s, meta_r, 0)
     mate = 1 - 2 * (c % 2)
     outer = -mate
@@ -321,8 +336,8 @@
         remote(here, here, aa_send.at[d], aa_recv.at[d], (s, (c + d) % nm)).wait_recv()
 
     settle(meta_near, meta_s, meta_r)
-    own_row = meta_ref[0:1, :] * SCALE
-    own_col = meta_ref[1:2, :] * SCALE
+    own_row = meta_near[4, 0:1, :] * SCALE
+    own_col = meta_near[4, 1:2, :] * SCALE
     lane = lax.broadcasted_iota(jnp.int32, (256, 128), 1).astype(F32) * SCALE
     log_norm = math.log2(nm * 32 - 1)
 
@@ -346,17 +361,9 @@
     lax.fori_loop(0, 9, taper_step, 0)
     noise_second()
     noise_third()
-    noise_settle()
-
-    def pre_step(p, carry):
-        m = meta_near[p]
-        pre_near[p] = m[3:4, :] + jnp.sqrt(m[4:5, :]) * noise_near[p].astype(F32)
-        return carry
-
-    lax.fori_loop(0, 9, pre_step, 0)
-
-    own_r = meta_ref[0:1, :]
-    own_c = meta_ref[1:2, :].astype(jnp.int32)
+
+    own_r = meta_near[4, 0:1, :]
+    own_c = meta_near[4, 1:2, :].astype(jnp.int32)
     row_b = jnp.broadcast_to(own_r, (32, 256))
     col_b = jnp.broadcast_to(own_c, (32, 256))
     for d in range(nm):
@@ -392,7 +399,7 @@
     for r in range(16):
         xp[r // 2, :, (r % 2) * 128:(r % 2) * 128 + 128] = slab_t[r]
 
-    variance = meta_ref[4:5, :]
+    variance = meta_near[4, 4:5, :]
 
     def near_step(p, own):
         m = meta_near[p]
@@ -400,7 +407,8 @@
         x = x_near[p].astype(F32)
         mean = jnp.sum(x, axis=0, keepdims=True) * (1.0 / 256.0)
         y = jnp.where(live, (x - mean).astype(BF16).astype(F32), 0.0)
-        b = jnp.where(live, pre_near[p] - x, 0.0)
+        pre = m[3:4, :] + jnp.sqrt(m[4:5, :]) * noise_near[p].astype(F32)
+        b = jnp.where(live, pre - x, 0.0)
         b_near[p] = b
         if own:
             y_own[...] = y.astype(BF16)
@@ -413,6 +421,7 @@
         return dot(b.astype(BF16), kt)
 
     acc = near_step(4, True)
+    noise_settle()
     settle(x_near, x_s, x_r)
 
     def near_loop(q, acc):
@@ -610,19 +619,6 @@
 
 def shards(ns, nm, prior, location, counts, datum, draws, spread):
     obs = location.shape[1] * location.shape[2]
-    cells = location.reshape(1, obs)
-    slot = jnp.arange(obs, dtype=jnp.int32)[None] % location.shape[2]
-    live = slot < jnp.repeat(counts.reshape(-1), location.shape[2])[None]
-    meta = jnp.concatenate(
-        [
-            (cells // 128).astype(F32),
-            (cells % 128).astype(F32),
-            live.astype(F32),
-            datum.reshape(1, obs),
-            spread.reshape(1, obs),
-            jnp.zeros((3, obs), F32),
-        ]
-    )
     noise = draws.reshape(draws.shape[1], obs)
     nz = ns // NX
     near = (9, 256, 256)
@@ -636,7 +632,6 @@
         pltpu.VMEM((9, 8, 256), F32),
         pltpu.VMEM(near, BF16),
         pltpu.VMEM(near, BF16),
-        pltpu.VMEM(near, F32),
         pltpu.VMEM(near, F32),
         pltpu.VMEM(near, BF16),
         pltpu.VMEM((256, 256), BF16),
@@ -687,6 +682,9 @@
         in_specs=[
             pl.BlockSpec(memory_space=pl.ANY),
             pl.BlockSpec(memory_space=pltpu.VMEM),
+            pl.BlockSpec(memory_space=pltpu.SMEM),
+            pl.BlockSpec(memory_space=pltpu.VMEM),
+            pl.BlockSpec(memory_space=pltpu.VMEM),
             pl.BlockSpec(memory_space=pltpu.VMEM),
         ],
         out_specs=pl.BlockSpec(memory_space=pltpu.VMEM),
@@ -694,7 +692,7 @@
         compiler_params=pltpu.CompilerParams(
             collective_id=0, has_side_effects=True, vmem_limit_bytes=60 * 1024 * 1024
         ),
-    )(prior, meta, noise)
+    )(prior, location, counts, datum, spread, noise)
 
 
 def solution(mesh):

time: 116 us -> 109 us (0.940)
  Pallas kernels: 109 us -> 105 us
  local copies, waits for them, and re-layouts: 6.56 us -> 3.88 us
    pallas_call x1, Pallas kernels: 109 us -> 105 us  [shards(): pl.pallas_call(functools.partial(body, ns, nm), out_shape=jax.ShapeDtypeS...]
    unnamed x10 -> x2, local copies, waits for them, and re-layouts: 5.88 us -> 3.88 us
where the time goes in v3:
time: 109 us
  Pallas kernels  105 us (96%)
  local copies, waits for them, and re-layouts  3.88 us (4%)
    pallas_call x1, Pallas kernels, shards(): pl.pallas_call(functools.partial(body, ns, nm), out_shape=jax.ShapeDtypeS...  105 us
    unnamed x2, local copies, waits for them, and re-layouts  3.88 us

profile of v3, /device:TPU:1, one launch (start us, length us, event | category | flops | bytes accessed | tf_op | source)
XLA Modules:
  0.0 108.9 jit_solution(1290389675254414427)
XLA Ops:
  0.0 1.6 %copy.9 = bf16[32,8,2,128]{3,1,2,0:T(8,128)(2,1)} copy(bf16[32,8,2,128]{3,2,1,0:T(2,128)(2,1)} %bitcast.6) | data formatting | bytes 262144
  1.6 105.0 %shard_map.64 = bf16[32,16,1024]{2,1,0:T(8,128)(2,1)} custom-call(bf16[32,16,1024]{2,1,0:T(8,128)(2,1)} %prior_ref.1, s32[1,2,128]{2,1,0:T(2,128)} %location_ref.1, s32[1,2]{1,0:T(1,128)} %count_ref.1, f32[1,2,128]{2,1,0:T(2,128)} %datum_ref.1, f32[1,2,128]{2,1,0:T(2,128)} %spread_ref.1, bf16[256,256]{1,0:T(8,128)(2,1)} %bitcast.5), custom_call_target="tpu_custom_call" | custom-call | tf_op jit(solution)/shard_map/pallas_call | solution.py:679
  106.6 2.3 %copy.11 = bf16[32,16,1024]{2,1,0:T(8,128)(2,1)} copy(bf16[32,16,1024]{2,1,0:T(8,128)(2,1)} %shard_map.64) | data formatting | bytes 2097152

commit v4 on v3

--- a/solution.py
+++ b/solution.py
@@ -421,16 +421,37 @@
         return dot(b.astype(BF16), kt)
 
     acc = near_step(4, True)
+    acc = lax.fori_loop(0, 2, lambda q, acc: acc + near_step(1 + 6 * q, False), acc)
     noise_settle()
     settle(x_near, x_s, x_r)
-
-    def near_loop(q, acc):
-        p = q + (q >= 4).astype(jnp.int32)
-        return acc + near_step(p, False)
-
-    acc = lax.fori_loop(0, 8, near_loop, acc)
+    acc = lax.fori_loop(
+        0, 6, lambda q, acc: acc + near_step(3 * (q // 2) + 2 * (q % 2), False), acc
+    )
     b_own = b_near[4]
     v1 = acc + (variance - SHIFT) * b_own
+
+    members = [(s, (c + d) % nm) for d in range(1, nm)]
+    along_x = [(((sx + d) % NX) * nz + sz, c) for d in range(1, NX)]
+    along_z = [(sx * nz + (sz + d) % nz, c) for d in range(1, nz)]
+
+    def spread(source, into, send, recv, devices):
+        for k, device in enumerate(devices):
+            send_if(True, functools.partial(
+                remote, source, into.at[k], send.at[k], recv.at[k], device
+            ))
+
+    def collect(own, into, send, recv, devices):
+        for k, device in enumerate(devices):
+            remote(into.at[k], into.at[k], send.at[k], recv.at[k], device).wait_recv()
+        for k in range(len(devices)):
+            own = own + into[k]
+        return own
+
+    def total_row(ref, k, prod):
+        half = prod[:, 0:128] + prod[:, 128:256]
+        row = jnp.sum(jnp.transpose(half), axis=0, keepdims=True)
+        ref[k:k + 1, :] = row[:, 0:128]
+        ref[k + 1:k + 2, :] = row[:, 128:256]
 
     def share(v, near, low, send, recv):
         high = v.astype(BF16)
@@ -457,73 +478,58 @@
 
         lax.fori_loop(low * 9, high * 9, step, 0)
 
+    def apply_mid(near, low):
+        acc = dot(low[1], k_t[4])
+        for p in (1, 4, 7):
+            acc = acc + dot(near[p], k_t[p])
+        return acc
+
+    def apply_rest(acc, near, low):
+        def step(q, acc):
+            p = 3 * (q // 2) + 2 * (q % 2)
+            return acc + dot(near[p], k_t[p])
+
+        acc = lax.fori_loop(0, 6, step, acc)
+        return acc + dot(low[0], k_t[1]) + dot(low[2], k_t[7])
+
     v1_own[...] = v1
+    b_own = b_near[4]
+    total_row(early.at[0], 0, b_own * b_own)
+    total_row(early.at[0], 2, b_own * v1)
+    total_row(early.at[0], 4, v1 * v1)
     weights(0, 1)
     forward(v1_near, v1_s, v1_r, 0)
     start_low(v1_low, v1_ls, v1_lr)
+    forward(v1_near, v1_s, v1_r, 1)
     weights(1, 2)
-    forward(v1_near, v1_s, v1_r, 1)
+    spread(early.at[0], early1, e1_s, e1_r, members)
     weights(2, 3)
+    acc = apply_mid(v1_near, v1_low)
     settle_low(v1_low, v1_ls, v1_lr)
     settle(v1_near, v1_s, v1_r)
 
-    def apply_near(near, low):
-        def step(p, acc):
-            return acc + dot(near[p], k_t[p])
-
-        acc = lax.fori_loop(0, 9, step, jnp.zeros((256, 256), F32))
-        for i in range(3):
-            acc = acc + dot(low[i], k_t[3 * i + 1])
-        return acc
-
-    v2 = apply_near(v1_near, v1_low) + (variance - SHIFT) * v1_own[...]
+    v2 = apply_rest(acc, v1_near, v1_low) + (variance - SHIFT) * v1_own[...]
     share(v2, v2_near, v2_low, v2_s, v2_r)
     v2_own[...] = v2
-    members = [(s, (c + d) % nm) for d in range(1, nm)]
-    along_x = [(((sx + d) % NX) * nz + sz, c) for d in range(1, NX)]
-    along_z = [(sx * nz + (sz + d) % nz, c) for d in range(1, nz)]
-
-    def spread(source, into, send, recv, devices):
-        for k, device in enumerate(devices):
-            send_if(True, functools.partial(
-                remote, source, into.at[k], send.at[k], recv.at[k], device
-            ))
-
-    def collect(own, into, send, recv, devices):
-        for k, device in enumerate(devices):
-            remote(into.at[k], into.at[k], send.at[k], recv.at[k], device).wait_recv()
-        for k in range(len(devices)):
-            own = own + into[k]
-        return own
-
-    def total_row(ref, k, prod):
-        half = prod[:, 0:128] + prod[:, 128:256]
-        row = jnp.sum(jnp.transpose(half), axis=0, keepdims=True)
-        ref[k:k + 1, :] = row[:, 0:128]
-        ref[k + 1:k + 2, :] = row[:, 128:256]
-
-    b_own = b_near[4]
     v1 = v1_own[...]
-    v2 = v2_own[...]
-    early[0] = jnp.zeros(early.shape[1:], F32)
-    for k, prod in enumerate((b_own * b_own, b_own * v1, v1 * v1, v1 * v2, v2 * v2)):
-        total_row(early.at[0], 2 * k, prod)
+    total_row(late.at[0], 0, v1 * v2)
+    total_row(late.at[0], 2, v2 * v2)
+    early[1] = collect(early[0], early1, e1_s, e1_r, members)
+    spread(early.at[1], early2, e2_s, e2_r, along_x)
     weights(3, 4)
     forward(v2_near, v2_s, v2_r, 0)
     start_low(v2_low, v2_ls, v2_lr)
-    spread(early.at[0], early1, e1_s, e1_r, members)
+    forward(v2_near, v2_s, v2_r, 1)
     weights(4, 5)
-    forward(v2_near, v2_s, v2_r, 1)
+    early[2] = collect(early[1], early2, e2_s, e2_r, along_x)
+    spread(early.at[2], early3, e3_s, e3_r, along_z)
     weights(5, 6)
-    early[1] = collect(early[0], early1, e1_s, e1_r, members)
-    spread(early.at[1], early2, e2_s, e2_r, along_x)
+    acc = apply_mid(v2_near, v2_low)
     settle_low(v2_low, v2_ls, v2_lr)
     settle(v2_near, v2_s, v2_r)
     v2 = v2_own[...]
-    total_row(late.at[0], 0, v2 * (apply_near(v2_near, v2_low) + (variance - SHIFT) * v2))
+    total_row(late.at[0], 4, v2 * (apply_rest(acc, v2_near, v2_low) + (variance - SHIFT) * v2))
     spread(late.at[0], late1, r1_s, r1_r, members)
-    early[2] = collect(early[1], early2, e2_s, e2_r, along_x)
-    spread(early.at[2], early3, e3_s, e3_r, along_z)
     weights(6, 7)
     late[1] = collect(late[0], late1, r1_s, r1_r, members)
     spread(late.at[1], late2, r2_s, r2_r, along_x)
@@ -533,7 +539,7 @@
     first = collect(early[2], early3, e3_s, e3_r, along_z)
     final = collect(late[2], late3, r3_s, r3_r, along_z)
 
-    mu = [first[2 * k:2 * k + 2] for k in range(5)] + [final]
+    mu = [rows[2 * k:2 * k + 2] for rows in (first, final) for k in range(3)]
 
     def inner(a, b):
         terms = [x * y * mu[i + j] for i, x in enumerate(a) for j, y in enumerate(b)]
@@ -650,14 +656,14 @@
         pltpu.VMEM((4, 256, 512), BF16),
         pltpu.VMEM((8, 4, 32, 512), BF16),
         pltpu.VMEM((8, 512, 128), F32),
-        pltpu.VMEM((3, 16, 128), F32),
-        pltpu.VMEM((7, 16, 128), F32),
-        pltpu.VMEM((NX - 1, 16, 128), F32),
-        pltpu.VMEM((nz - 1, 16, 128), F32),
-        pltpu.VMEM((3, 2, 128), F32),
-        pltpu.VMEM((7, 2, 128), F32),
-        pltpu.VMEM((NX - 1, 2, 128), F32),
-        pltpu.VMEM((nz - 1, 2, 128), F32),
+        pltpu.VMEM((3, 6, 128), F32),
+        pltpu.VMEM((7, 6, 128), F32),
+        pltpu.VMEM((NX - 1, 6, 128), F32),
+        pltpu.VMEM((nz - 1, 6, 128), F32),
+        pltpu.VMEM((3, 6, 128), F32),
+        pltpu.VMEM((7, 6, 128), F32),
+        pltpu.VMEM((NX - 1, 6, 128), F32),
+        pltpu.VMEM((nz - 1, 6, 128), F32),
         dma((8,)), dma((8,)),
         dma((9, 1)), dma((9, 1)),
         dma((9, 1)), dma((9, 1)),

time: 109 us -> 107 us (0.982)
  Pallas kernels: 105 us -> 103 us
    pallas_call x1, Pallas kernels: 105 us -> 103 us  [shards(): pl.pallas_call(functools.partial(body, ns, nm), out_shape=jax.ShapeDtypeS...]
where the time goes in v4:
time: 107 us
  Pallas kernels  103 us (96%)
  local copies, waits for them, and re-layouts  3.88 us (4%)
    pallas_call x1, Pallas kernels, shards(): pl.pallas_call(functools.partial(body, ns, nm), out_shape=jax.ShapeDtypeS...  103 us
    unnamed x2, local copies, waits for them, and re-layouts  3.88 us

profile of v4, /device:TPU:1, one launch (start us, length us, event | category | flops | bytes accessed | tf_op | source)
XLA Modules:
  0.0 107.0 jit_solution(6673102286688202858)
XLA Ops:
  0.0 1.6 %copy.9 = bf16[32,8,2,128]{3,1,2,0:T(8,128)(2,1)} copy(bf16[32,8,2,128]{3,2,1,0:T(2,128)(2,1)} %bitcast.6) | data formatting | bytes 262144
  1.6 103.2 %shard_map.64 = bf16[32,16,1024]{2,1,0:T(8,128)(2,1)} custom-call(bf16[32,16,1024]{2,1,0:T(8,128)(2,1)} %prior_ref.1, s32[1,2,128]{2,1,0:T(2,128)} %location_ref.1, s32[1,2]{1,0:T(1,128)} %count_ref.1, f32[1,2,128]{2,1,0:T(2,128)} %datum_ref.1, f32[1,2,128]{2,1,0:T(2,128)} %spread_ref.1, bf16[256,256]{1,0:T(8,128)(2,1)} %bitcast.5), custom_call_target="tpu_custom_call" | custom-call | tf_op jit(solution)/shard_map/pallas_call | solution.py:685
  104.7 2.3 %copy.11 = bf16[32,16,1024]{2,1,0:T(8,128)(2,1)} copy(bf16[32,16,1024]{2,1,0:T(8,128)(2,1)} %shard_map.64) | data formatting | bytes 2097152

commit v5 on v4

--- a/solution.py
+++ b/solution.py
@@ -264,10 +264,6 @@
             if j == 0:
                 v1_low[1 + i] = jnp.zeros(v1_low.shape[1:], BF16)
                 v2_low[1 + i] = jnp.zeros(v2_low.shape[1:], BF16)
-    for d in range(1, nm):
-        pack(d).wait()
-    pl.semaphore_wait(barrier, count)
-
     def flat(ref):
         return jnp.concatenate([ref[0, 0:1, :], ref[0, 1:2, :]], axis=1)
 
@@ -283,6 +279,10 @@
     meta_near[4, 4:5, :] = flat(spread_ref)
     meta_near[4, 5:8, :] = jnp.zeros((3, 256), F32)
     noise_near[4] = noise_ref[...]
+    for d in range(1, nm):
+        pack(d).wait()
+    pl.semaphore_wait(barrier, count)
+
     start(meta_near, meta_s, meta_r)
     for j in (-1, 1):
         halo(noise_near.at[4], noise_near, noise_s, noise_r, 0, j, 0)
@@ -331,8 +331,8 @@
             noise_landed(exists(i, 0), i, mate)
             noise_landed(jnp.logical_and(exists(i, 0), has_outer), i, outer)
 
-    def piece_wait(d):
-        here = slab.at[pl.ds(((c + nm - d) % nm) * 32, 32)]
+    def piece_wait(d, source):
+        here = slab.at[pl.ds(source * 32, 32)]
         remote(here, here, aa_send.at[d], aa_recv.at[d], (s, (c + d) % nm)).wait_recv()
 
     settle(meta_near, meta_s, meta_r)
@@ -366,13 +366,15 @@
     own_c = meta_near[4, 1:2, :].astype(jnp.int32)
     row_b = jnp.broadcast_to(own_r, (32, 256))
     col_b = jnp.broadcast_to(own_c, (32, 256))
-    for d in range(nm):
-        if d == 0:
+    for source in range(nm):
+        @pl.when(c == source)
+        def _():
             own_piece.wait()
-        else:
-            piece_wait(d)
-        source = (c + nm - d) % nm
-        base = pl.multiple_of(source * 32, 32)
+
+        @pl.when(c != source)
+        def _():
+            piece_wait((c + nm - source) % nm, source)
+        base = source * 32
         part[...] = slab[pl.ds(base, 32)].astype(F32).reshape(512, 128)
         for half in range(2):
             sl = slice(half * 128, half * 128 + 128)
@@ -384,7 +386,9 @@
                 g = jnp.take_along_axis(v, col_b[:, sl], axis=1, mode="promise_in_bounds")
                 got = jnp.where(row_b[:, sl] == float(r), g, got)
             x_near[4, pl.ds(base, 32), sl] = got.astype(BF16)
-    start(x_near, x_s, x_r)
+        if (source + 1) % (nm // 2) == 0:
+            for i, j in ((-1, 0), (1, 0), (0, -1), (0, 1)):
+                halo(x_near.at[4], x_near, x_s, x_r, i, j, source // (nm // 2))
 
     def xp_step(r, carry):
         x = slab_t[r].astype(F32)

time: 107 us -> 106 us (level)
    pallas_call x1, Pallas kernels: 103 us -> 102 us  [shards(): pl.pallas_call(functools.partial(body, ns, nm), out_shape=jax.ShapeDtypeS...]
where the time goes in v5:
time: 106 us
  Pallas kernels  102 us (96%)
  local copies, waits for them, and re-layouts  3.88 us (4%)
    pallas_call x1, Pallas kernels, shards(): pl.pallas_call(functools.partial(body, ns, nm), out_shape=jax.ShapeDtypeS...  102 us
    unnamed x2, local copies, waits for them, and re-layouts  3.88 us

profile of v5, /device:TPU:1, one launch (start us, length us, event | category | flops | bytes accessed | tf_op | source)
XLA Modules:
  0.0 105.9 jit_solution(7757017886779825398)
XLA Ops:
  0.0 1.6 %copy.9 = bf16[32,8,2,128]{3,1,2,0:T(8,128)(2,1)} copy(bf16[32,8,2,128]{3,2,1,0:T(2,128)(2,1)} %bitcast.6) | data formatting | bytes 262144
  1.6 102.0 %shard_map.64 = bf16[32,16,1024]{2,1,0:T(8,128)(2,1)} custom-call(bf16[32,16,1024]{2,1,0:T(8,128)(2,1)} %prior_ref.1, s32[1,2,128]{2,1,0:T(2,128)} %location_ref.1, s32[1,2]{1,0:T(1,128)} %count_ref.1, f32[1,2,128]{2,1,0:T(2,128)} %datum_ref.1, f32[1,2,128]{2,1,0:T(2,128)} %spread_ref.1, bf16[256,256]{1,0:T(8,128)(2,1)} %bitcast.5), custom_call_target="tpu_custom_call" | custom-call | tf_op jit(solution)/shard_map/pallas_call | solution.py:689
  103.6 2.3 %copy.11 = bf16[32,16,1024]{2,1,0:T(8,128)(2,1)} copy(bf16[32,16,1024]{2,1,0:T(8,128)(2,1)} %shard_map.64) | data formatting | bytes 2097152
